TPU v7x, 32 devices: a whole 2x2x4 slice. The times are simulated.
32 devices in a mesh: dp: 2 (over x), group: 4 (over z), head: 4 (over y, core).
Axes of the slice: x: 2, y: 2, z: 4, core: 2. Of those that a mesh axis runs over, the one named last changes fastest.
Arguments:
- query: bfloat16 [1024, 2048], P('dp', ('group', 'head')), parts along dimension 0, may hold values from -200 to 200
- query_exp: int32 [64, 1024], P(('group', 'head'), 'dp'), parts along dimension 1, may hold values from -1 to 0
- kv: bfloat16 [1024, 1024], P('dp', 'group'), parts along dimension 0, may hold values from -10 to 10
- kv_exp: int32 [32, 1024], P('group', 'dp'), parts along dimension 1, may hold values from -2 to 2, as said below
- out_grad: bfloat16 [1024, 2048], P('dp', ('group', 'head')), parts along dimension 0, may hold values from -6 to 6
- out_grad_exp: int32 [64, 1024], P(('group', 'head'), 'dp'), parts along dimension 1, may hold values from -2 to 2
- q_weight: bfloat16 [4096, 2048], P('dp', ('group', 'head')), parts along dimension 0, may hold values from -0.1875 to 0.1875
- q_weight_exp: int32 [128, 2048], P('dp', ('group', 'head')), parts along dimension 0, may hold values from -1 to 1
- keyvalue_weight_mantissa: bfloat16 [4096, 1024], P(('dp', 'head'), 'group'), parts along dimension 0, may hold values from -0.375 to 0.375
- keyvalue_weight_exponent: int32 [128, 1024], P(('dp', 'head'), 'group'), parts along dimension 0, may hold values from -1 to 1
Outputs:
- input_grad: bfloat16 [1024, 2048], P(('dp', 'head'), 'group'), parts along dimension 0
- keyvalue_gradient: bfloat16 [1024, 1024], P(('dp', 'head'), 'group'), parts along dimension 0
There are 2 independent parts, one for each index of `dp`. A program takes and returns all parts, laid end to end along the dimension named above; each array names one. Nothing has to cross between parts.
Inputs may be any that keep to these rules, and one draw needn't show every extreme that they name: `kv_exp`: exponents of the key blocks lie in -1 to 0, those of the value blocks in -2 to 2.
All inputs are finite; a program needn't handle non-finite values.
Results may differ from a plain program's by a relative error of at most 0.022.
Values may be sent and summed in bfloat16 or wider, within the bound.
A program may use at most 64 MiB of HBM per device.

v0:
```python
import jax
import jax.numpy as jnp
from jax import lax
from jax.sharding import PartitionSpec as P


def power_of_two(block_exponent):
    scale_lookup = jnp.zeros(block_exponent.shape, jnp.float32)
    for level in range(-4, 5):
        scale_lookup = scale_lookup + jnp.where(block_exponent == level, 2.0**level, 0.0).astype(
            jnp.float32
        )
    return scale_lookup


def dequant_rows(mantissa, block_exponent):
    scaling = jnp.repeat(power_of_two(block_exponent).T, 32, axis=1)
    return (mantissa.astype(jnp.float32) * scaling).astype(jnp.bfloat16)


def dequant_cols(mantissa, block_exponent):
    scaling = jnp.repeat(power_of_two(block_exponent), 32, axis=0)
    return (mantissa.astype(jnp.float32) * scaling).astype(jnp.bfloat16)


def shards(
    query,
    query_exp,
    kv,
    kv_exp,
    out_grad,
    out_grad_exp,
    q_weight,
    q_weight_exp,
    keyvalue_weight_mantissa,
    keyvalue_weight_exponent,
):
    seq_len = query.shape[0]
    head_dim = query.shape[1]
    scale = 1.0 / head_dim**0.5
    q_local = dequant_rows(query, query_exp)
    kv_local = dequant_rows(kv, kv_exp)
    do_local = dequant_rows(out_grad, out_grad_exp)
    keys = kv_local[:, :head_dim]
    value_matrix = kv_local[:, head_dim:]
    block = min(512, seq_len)
    blocks = seq_len // block
    dq_parts = []
    dk_accum = jnp.zeros((seq_len, head_dim), jnp.float32)
    dv_accum = jnp.zeros((seq_len, head_dim), jnp.float32)
    for index in range(blocks):
        first = index * block
        upper = first + block
        q_block = q_local[first:upper]
        do_block = do_local[first:upper]
        key_rows = keys[:upper]
        value_rows = value_matrix[:upper]
        scores = (
            lax.dot_general(
                q_block, key_rows, (((1,), (1,)), ((), ())), preferred_element_type=jnp.float32
            )
            * scale
        )
        row_pos = first + jnp.arange(block, dtype=jnp.int32)[:, None]
        col_pos = jnp.arange(upper, dtype=jnp.int32)[None, :]
        scores = jnp.where(col_pos <= row_pos, scores, -jnp.inf)
        peak = jnp.max(scores, axis=1, keepdims=True)
        expd = jnp.exp(scores - peak)
        probs = expd / jnp.sum(expd, axis=1, keepdims=True)
        probs_b = probs.astype(jnp.bfloat16)
        output = jnp.dot(probs_b, value_rows, preferred_element_type=jnp.float32)
        delta = jnp.sum(do_block.astype(jnp.float32) * output, axis=1, keepdims=True)
        dprob = lax.dot_general(
            do_block, value_rows, (((1,), (1,)), ((), ())), preferred_element_type=jnp.float32
        )
        dscore = (probs * (dprob - delta) * scale).astype(jnp.bfloat16)
        dq_parts.append(
            jnp.dot(dscore, key_rows, preferred_element_type=jnp.float32).astype(jnp.bfloat16)
        )
        dk_accum = dk_accum.at[:upper].add(
            lax.dot_general(
                dscore, q_block, (((0,), (0,)), ((), ())), preferred_element_type=jnp.float32
            )
        )
        dv_accum = dv_accum.at[:upper].add(
            lax.dot_general(
                probs_b, do_block, (((0,), (0,)), ((), ())), preferred_element_type=jnp.float32
            )
        )
    dq_local = jnp.concatenate(dq_parts, axis=0)
    dkv_local = jnp.concatenate(
        [dk_accum.astype(jnp.bfloat16), dv_accum.astype(jnp.bfloat16)], axis=1
    )
    packed = jnp.concatenate([dq_local, dkv_local], axis=1)[:, None, :]
    moved = lax.all_to_all(packed, "head", split_axis=0, concat_axis=1, tiled=True)
    tok_rows = moved.shape[0]
    sources = moved.shape[1]
    dq_tokens = moved[:, :, :head_dim].reshape(tok_rows, sources * head_dim)
    kv_sum = jnp.sum(moved[:, :, head_dim:].astype(jnp.float32), axis=1)
    keyvalue_gradient = kv_sum.astype(jnp.bfloat16)
    w_query = dequant_cols(q_weight, q_weight_exp)
    total = lax.dot_general(
        dq_tokens,
        lax.all_gather(w_query, "head", axis=1, tiled=True),
        (((1,), (1,)), ((), ())),
        preferred_element_type=jnp.float32,
    )
    w_keyval = dequant_cols(keyvalue_weight_mantissa, keyvalue_weight_exponent)
    whole_keyval = lax.all_gather(w_keyval, "head", axis=0, tiled=True)
    total = total + lax.dot_general(
        keyvalue_gradient,
        whole_keyval,
        (((1,), (1,)), ((), ())),
        preferred_element_type=jnp.float32,
    )
    input_grad = lax.psum_scatter(
        total.astype(jnp.bfloat16), "group", scatter_dimension=1, tiled=True
    )
    return (input_grad, keyvalue_gradient)


def solution(mesh):
    return jax.shard_map(
        shards,
        mesh=mesh,
        in_specs=(
            P("dp", ("group", "head")),
            P(("group", "head"), "dp"),
            P("dp", "group"),
            P("group", "dp"),
            P("dp", ("group", "head")),
            P(("group", "head"), "dp"),
            P("dp", ("group", "head")),
            P("dp", ("group", "head")),
            P(("dp", "head"), "group"),
            P(("dp", "head"), "group"),
        ),
        out_specs=(P(("dp", "head"), "group"), P(("dp", "head"), "group")),
        check_vma=False,
    )
```

profile of v0, /device:TPU:0, one launch (start us, length us, event | category | flops | bytes accessed | tf_op | source)
XLA Modules:
  0.0 88.7 jit_solution(13513982982213977385)
XLA Ops:
  7.2 0.0 copy-start.4
  7.2 0.0 copy-start.1
  7.2 0.0 copy-start.2
  7.2 0.0 copy-start.3
  7.2 0.0 copy-start.5
  7.2 0.0 all-gather.5.cloned.1.call-start
  7.3 0.8 select_add_fusion.1
  8.1 0.0 copy-start.6
  8.1 1.7 %fusion.9 = bf16[512,256]{1,0:T(8,128)(2,1)} fusion(bf16[512,256]{1,0:T(8,128)(2,1)} %param.26, f32[16,256]{1,0:T(8,128)S(1)} %select_add_fusion.1), kind=kLoop, calls=%fused_computation.20 | loop fusion | flops 393216 | bytes 540672 | tf_op jit(solution)/shard_map/convert_element_type | solution.py:23
  9.8 0.0 all-gather.5.cloned.1.call-update
  9.8 0.0 all-gather.3.cloned.1.call-start
  9.9 0.8 select_add_fusion
  10.7 1.9 %fusion.6 = bf16[2048,128]{1,0:T(8,128)(2,1)} fusion(bf16[2048,128]{1,0:T(8,128)(2,1)} %param.24, f32[64,128]{1,0:T(8,128)S(1)} %select_add_fusion), kind=kLoop, calls=%fused_computation.14 | loop fusion | flops 786432 | bytes 1081344 | tf_op jit(solution)/shard_map/convert_element_type | solution.py:23
  12.6 0.0 all-gather.3.cloned.1.call-update
  12.6 0.0 reduce-scatter.2.cloned.1.call-start
  12.7 0.0 copy-done.4
  12.7 0.0 copy-done.1
  12.7 0.1 copy.28
  12.9 0.0 copy-done.2
  12.9 0.1 copy.27
  13.0 0.0 copy-done.3
  13.0 0.1 copy.29
  13.2 0.0 copy-done.5
  13.3 0.0 copy-done.6
  13.3 0.4 fusion.18
  13.7 0.2 fusion.8
  13.9 0.2 fusion.11
  14.1 0.2 fusion.5
  14.3 0.4 fusion.4
  14.7 0.2 convolution_convert_fusion
  14.9 0.3 convolution_convert_fusion.2
  15.3 0.3 convolution_convert_fusion.1
  15.6 0.5 broadcast.102
  16.1 0.9 %reduce.7 = bf16[512,384]{0,1:T(8,128)(2,1)S(1)} reduce(bf16[512,1,384]{0,2,1:T(8,128)(2,1)S(1)} %maximum_bitcast_fusion, bf16[]{:T(256)} %broadcast.102), dimensions={1}, to_apply=%copy.31.reduce_sub_computation | reduce | bytes 786434 | tf_op jit(solution)/shard_map/broadcast_in_dim | solution.py:94
  17.1 0.2 copy.38
  17.3 0.1 reshape.81
  17.4 14.7 %all_to_all.18 = bf16[4,2,24576]{2,1,0:T(2,128)(2,1)S(1)} all-to-all(bf16[4,2,24576]{2,1,0:T(2,128)(2,1)S(1)} %reshape.81), channel_id=1, replica_groups=mesh['dp'=2,'group'=4,'head'=4] {'head'}, dimensions={0} | all-to-all | bytes 786432 | tf_op jit(solution)/shard_map/all_to_all | solution.py:95
  32.1 0.4 reshape.82
  32.5 0.1 copy.36
  32.6 0.1 copy.32
  32.8 0.0 copy-start
  32.8 0.0 all-gather.5.cloned.1.call-done
  32.9 1.7 %fusion.19 = f32[128,2048]{1,0:T(8,128)S(1)} fusion(bf16[128,256]{1,0:T(8,128)(2,1)S(1)} %slice_reduce_fusion, bf16[2048,256]{1,0:T(8,128)(2,1)} %all-gather.5.cloned.1.call-done), kind=kOutput, calls=%fused_computation.40 | convolution fusion | flops 134217728 | bytes 2162688 | tf_op jit(solution)/shard_map/dot_general | solution.py:110
  34.6 22.6 %all-gather.3.cloned.1.call-done = bf16[2048,512]{1,0:T(8,128)(2,1)} async-done(((bf16[2048,128]{1,0:T(8,128)(2,1)}), bf16[2048,512]{1,0:T(8,128)(2,1)}) %all-gather.3.cloned.1.call-update) | async-done | bytes 2097168 | tf_op jit(solution)/shard_map/all_gather | solution.py:104
  57.1 3.2 %fusion = bf16[128,2048]{1,0:T(8,128)(2,1)} fusion(f32[128,2048]{1,0:T(8,128)S(1)} %fusion.19, bf16[128,512]{0,1:T(8,128)(2,1)S(1)} %bitcast.48, bf16[2048,512]{1,0:T(8,128)(2,1)} %all-gather.3.cloned.1.call-done), kind=kOutput, calls=%fused_computation.1 | convolution fusion | flops 268959744 | bytes 3801088 | tf_op jit(solution)/shard_map/dot_general | solution.py:102
  60.4 0.0 copy-done
  60.4 0.0 reduce-scatter.2.cloned.1.call-update
  60.4 21.8 %reduce-scatter.2.cloned.1.call-done = bf16[128,512]{1,0:T(8,128)(2,1)} async-done(((bf16[128,2048]{1,0:T(8,128)(2,1)}), bf16[128,512]{1,0:T(8,128)(2,1)}) %reduce-scatter.2.cloned.1.call-update) | async-done | bytes 131088 | tf_op jit(solution)/shard_map/reduce_scatter | solution.py:116
  (9 shorter events, 0.3 us)
Async XLA Ops:
  7.2 5.5 %copy-start.4 = (s32[8,512]{1,0:T(8,128)S(1)}, s32[8,512]{1,0:T(8,128)}, u32[]{:S(2)}) copy-start(s32[8,512]{1,0:T(8,128)} %param.21) | copy-start | bytes 49156
  7.2 5.5 %copy-start.1 = (bf16[512,256]{1,0:T(8,128)(2,1)S(1)}, bf16[512,256]{1,0:T(8,128)(2,1)}, u32[]{:S(2)}) copy-start(bf16[512,256]{1,0:T(8,128)(2,1)} %param.20) | copy-start | bytes 786436
  7.2 5.7 %copy-start.2 = (bf16[512,128]{1,0:T(8,128)(2,1)S(1)}, bf16[512,128]{1,0:T(8,128)(2,1)}, u32[]{:S(2)}) copy-start(bf16[512,128]{1,0:T(8,128)(2,1)} %param.18) | copy-start | bytes 393220
  7.2 5.8 %copy-start.3 = (bf16[512,128]{1,0:T(8,128)(2,1)S(1)}, bf16[512,128]{1,0:T(8,128)(2,1)}, u32[]{:S(2)}) copy-start(bf16[512,128]{1,0:T(8,128)(2,1)} %param.22) | copy-start | bytes 393220
  7.2 6.0 %copy-start.5 = (s32[4,512]{1,0:T(4,128)S(1)}, s32[4,512]{1,0:T(4,128)}, u32[]{:S(2)}) copy-start(s32[4,512]{1,0:T(4,128)} %param.19) | copy-start | bytes 24580
  7.2 25.6 %all-gather.5.cloned.1.call-start = ((), (), s32[]{:S(2)}) async-start(), calls=%async_computation.3 | async-start | bytes 1310720 | tf_op jit(solution)/shard_map/all_gather | solution.py:109
  8.1 5.2 %copy-start.6 = (s32[4,512]{1,0:T(4,128)S(1)}, s32[4,512]{1,0:T(4,128)}, u32[]{:S(2)}) copy-start(s32[4,512]{1,0:T(4,128)} %param.23) | copy-start | bytes 24580
  9.8 47.3 %all-gather.3.cloned.1.call-start = ((), (), s32[]{:S(2)}) async-start(), calls=%async_computation.2 | async-start | bytes 2621440 | tf_op jit(solution)/shard_map/all_gather | solution.py:104
  12.6 69.6 %reduce-scatter.2.cloned.1.call-start = ((), (), s32[]{:S(2)}) async-start(), calls=%async_computation.4 | async-start | bytes 655360 | tf_op jit(solution)/shard_map/reduce_scatter | solution.py:116
  32.8 27.5 %copy-start = (bf16[128,256]{1,0:T(8,128)(2,1)}, bf16[128,256]{1,0:T(8,128)(2,1)S(1)}, u32[]{:S(2)}) copy-start(bf16[128,256]{1,0:T(8,128)(2,1)S(1)} %slice_reduce_fusion) | copy-start | bytes 196612
Sparse Core Ops, SparseCore 0:
  9.9 22.7 all-gather.4
  34.3 22.8 all-gather.2
  60.5 21.6 reduce-scatter.1
where the time goes:
time: 89.1 us; the launch traced here: 88.7 us
  waiting for transfers between devices  44.5 us (50%)
  blocking collectives  14.7 us (16%)
  between operations  14 us (16%)
  other arithmetic  6.77 us (8%)
  matrix products  6.76 us (8%)
  local copies, waits for them, and re-layouts  1.85 us (2%)
    all_gather x1, waiting for transfers between devices, shards(): lax.all_gather(w_query, 'head', axis=1, tiled=True)  22.6 us
    reduce_scatter x1, waiting for transfers between devices, shards(): lax.psum_scatter(total.astype(jnp.bfloat16), 'group', scatter_dimension=1...  21.8 us
    all_to_all x1, blocking collectives, shards(): lax.all_to_all(packed, 'head', split_axis=0, concat_axis=1, tiled=True)  14.7 us
    convert_element_type x2, other arithmetic, dequant_cols(): return (mantissa.astype(jnp.float32) * scaling).astype(jnp.bfloat16)  3.64 us
    dot_general x1, matrix products, shards(): lax.dot_general(dq_tokens, lax.all_gather(w_query, 'head', axis=1, tiled=...  3.21 us
  transfers between devices with their start and end apart: 3, of which 2 were waited for; matrix products, arithmetic and copies ran while one was open for 11% of the time, Pallas kernels for 0%

commit v1 on v0

v1 whole, which is shorter than its diff:
```python
import functools

import jax
import jax.numpy as jnp
from jax import lax
from jax.experimental import pallas as pl
from jax.experimental.pallas import tpu as pltpu
from jax.sharding import PartitionSpec as P

MESH = pl.DeviceIdType.MESH
F32 = jnp.float32
BF16 = jnp.bfloat16
CORES = 2
BLOCK = 32


def power_of_two(exponent):
    scale = jnp.where(exponent == 0, 1.0, 0.0)
    for level in (-4, -3, -2, -1, 1, 2, 3, 4):
        scale = jnp.where(exponent == level, 2.0**level, scale)
    return scale.astype(F32)


def dequant_rows(mantissa, exponent):
    blocks, rows = exponent.shape
    scale = jnp.broadcast_to(power_of_two(exponent)[:, None, :], (blocks, BLOCK, rows))
    scale = scale.reshape(blocks * BLOCK, rows).T
    return (mantissa.astype(F32) * scale).astype(BF16)


def dequant_cols(mantissa, exponent):
    blocks, columns = exponent.shape
    scale = jnp.broadcast_to(power_of_two(exponent)[:, None, :], (blocks, BLOCK, columns))
    return (mantissa.astype(F32) * scale.reshape(blocks * BLOCK, columns)).astype(BF16)


def dot_nt(a, b):
    return lax.dot_general(a, b, (((1,), (1,)), ((), ())), preferred_element_type=F32)


def dot_tn(a, b):
    return lax.dot_general(a, b, (((0,), (0,)), ((), ())), preferred_element_type=F32)


def kernel(
    groups,
    heads,
    q_ref,
    qe_ref,
    kv_ref,
    kve_ref,
    do_ref,
    doe_ref,
    wq_ref,
    wqe_ref,
    wkv_ref,
    wkve_ref,
    out_ref,
    kvg_ref,
    wq_pair,
    wq_out,
    wkv_half,
    wkv_out,
    dq_pair,
    dkv_out,
    dkv_in,
    kvg_pair,
    part_out,
    part_in,
    z_out,
    z_in,
    dk_acc,
    dv_acc,
    w_sem,
    wkv_send,
    wkv_recv,
    dq_sem,
    dkv_send,
    dkv_recv,
    kvg_sem,
    part_send,
    part_recv,
    z_send,
    z_recv,
):
    seq, size = q_ref.shape
    model = wq_ref.shape[0]
    chips = heads // CORES
    tokens = seq // heads
    wide = model // groups
    half = model // CORES
    per_half = groups // CORES
    rows = wkv_ref.shape[0]
    owners = heads // CORES
    scale = 1.0 / size**0.5

    z = lax.axis_index("group")
    h = lax.axis_index("head")
    y = h // CORES
    c = lax.rem(h, CORES)
    sibling = y * CORES + (1 - c)

    barrier = pltpu.get_barrier_semaphore()
    for k in range(1, heads):
        pl.semaphore_signal(
            barrier, inc=1, device_id={"head": lax.rem(h + k, heads)}, device_id_type=MESH
        )
    for k in range(1, groups):
        for core in range(CORES):
            pl.semaphore_signal(
                barrier,
                inc=1,
                device_id={"group": lax.rem(z + k, groups), "head": y * CORES + core},
                device_id_type=MESH,
            )

    def weight_rows(which):
        first = pl.multiple_of(which * half, half)
        first_e = pl.multiple_of(which * (half // BLOCK), half // BLOCK)
        return dequant_cols(
            wq_ref[pl.ds(first, half), :], wqe_ref[pl.ds(first_e, half // BLOCK), :]
        )

    wq_out[...] = weight_rows(1 - c)
    wkv_out[...] = dequant_cols(wkv_ref[...], wkve_ref[...])
    pl.semaphore_wait(barrier, heads - 1 + CORES * (groups - 1))

    my_half = h // owners
    my_slot = pl.multiple_of(lax.rem(h, owners) * rows, rows)

    def wkv_copy(j):
        return pltpu.make_async_remote_copy(
            src_ref=wkv_out,
            dst_ref=wkv_half.at[pl.ds(my_slot, rows)],
            send_sem=wkv_send.at[j],
            recv_sem=wkv_recv.at[lax.rem(h, owners)],
            device_id={"head": CORES * j + my_half},
            device_id_type=MESH,
        )

    for j in range(owners):

        @pl.when(CORES * j + my_half != h)
        def _():
            wkv_copy(j).start()

    w_copy = pltpu.make_async_remote_copy(
        src_ref=wq_out,
        dst_ref=wq_pair.at[:, size:],
        send_sem=w_sem.at[0],
        recv_sem=w_sem.at[1],
        device_id={"head": sibling},
        device_id_type=MESH,
    )
    w_copy.start()
    wq_pair[:, :size] = weight_rows(c)

    @pl.when(my_half == c)
    def _():
        wkv_half[pl.ds(my_slot, rows), :] = wkv_out[...]

    query = dequant_rows(q_ref[...], qe_ref[...])
    kv = dequant_rows(kv_ref[...], kve_ref[...])
    grad = dequant_rows(do_ref[...], doe_ref[...])
    keys, values = kv[:, :size], kv[:, size:]
    block = min(256, seq)
    for index in reversed(range(seq // block)):
        first, upper = index * block, (index + 1) * block
        q_block, do_block = query[first:upper], grad[first:upper]
        scores = dot_nt(keys[:upper], q_block)
        key_at = lax.broadcasted_iota(jnp.int32, (upper, block), 0)
        query_at = first + lax.broadcasted_iota(jnp.int32, (upper, block), 1)
        scores = jnp.where(key_at <= query_at, scores, -jnp.inf)
        expd = jnp.exp((scores - jnp.max(scores, axis=0, keepdims=True)) * scale)
        probs = expd * (1.0 / jnp.sum(expd, axis=0, keepdims=True))
        probs_b = probs.astype(BF16)
        dprob = dot_nt(values[:upper], do_block)
        delta = jnp.sum(probs_b.astype(F32) * dprob, axis=0, keepdims=True)
        dscore = (probs * (dprob - delta) * scale).astype(BF16)
        dq_pair[first:upper, :size] = dot_tn(dscore, keys[:upper]).astype(BF16)
        dk = jnp.dot(dscore, q_block, preferred_element_type=F32)
        dv = jnp.dot(probs_b, do_block, preferred_element_type=F32)
        if upper == seq:
            dk_acc[...] = dk
            dv_acc[...] = dv
        else:
            dk_acc[:upper, :] += dk
            dv_acc[:upper, :] += dv

    dq_copy = pltpu.make_async_remote_copy(
        src_ref=dq_pair.at[:, :size],
        dst_ref=dq_pair.at[:, size:],
        send_sem=dq_sem.at[0],
        recv_sem=dq_sem.at[1],
        device_id={"head": sibling},
        device_id_type=MESH,
    )
    dq_copy.start()
    dkv_out[:, :size] = dk_acc[...].astype(BF16)
    dkv_out[:, size:] = dv_acc[...].astype(BF16)
    dkv_copies = []
    for k in range(1, heads):
        to = lax.rem(h + k, heads)
        copy = pltpu.make_async_remote_copy(
            src_ref=dkv_out.at[pl.ds(pl.multiple_of(to * tokens, tokens), tokens)],
            dst_ref=dkv_in.at[k - 1],
            send_sem=dkv_send.at[k - 1],
            recv_sem=dkv_recv.at[k - 1],
            device_id={"head": to},
            device_id_type=MESH,
        )
        copy.start()
        dkv_copies.append(copy)

    def q_term(chip, b, core):
        first = pl.multiple_of((chip * CORES + core) * tokens, tokens)
        at = pl.multiple_of(b * wide, wide)
        return dot_nt(dq_pair[pl.ds(first, tokens), :], wq_pair[pl.ds(at, wide), :])

    w_copy.wait_recv()
    dq_copy.wait_recv()
    chunks = [(i, core) for i in range(per_half) for core in range(CORES)]
    part_copies = {}
    for i, core in chunks:
        b = lax.rem(z + 1 + i, per_half)
        for k in range(1, chips):
            to = lax.rem(y + k, chips)
            part_out[k - 1, i, core] = q_term(to, b, core).astype(BF16)
            copy = pltpu.make_async_remote_copy(
                src_ref=part_out.at[k - 1, i, core],
                dst_ref=part_in.at[k - 1, i, core],
                send_sem=part_send.at[k - 1, i, core],
                recv_sem=part_recv.at[k - 1, i, core],
                device_id={"head": to * CORES + c},
                device_id_type=MESH,
            )
            copy.start()
            part_copies[k, i, core] = copy

    total = dkv_out[pl.ds(pl.multiple_of(h * tokens, tokens), tokens), :].astype(F32)
    for k in range(1, heads):
        dkv_copies[k - 1].wait_recv()
        total = total + dkv_in[k - 1].astype(F32)
    kvg = total.astype(BF16)
    kvg_ref[...] = kvg
    kvg_pair[c] = kvg
    kvg_copy = pltpu.make_async_remote_copy(
        src_ref=kvg_pair.at[c],
        dst_ref=kvg_pair.at[c],
        send_sem=kvg_sem.at[0],
        recv_sem=kvg_sem.at[1],
        device_id={"head": sibling},
        device_id_type=MESH,
    )
    kvg_copy.start()
    for s in range(owners):

        @pl.when(c * owners + s != h)
        def _():
            pltpu.make_async_remote_copy(
                src_ref=wkv_out,
                dst_ref=wkv_half.at[pl.ds(s * rows, rows)],
                send_sem=wkv_send.at[s],
                recv_sem=wkv_recv.at[s],
                device_id={"head": sibling},
                device_id_type=MESH,
            ).wait_recv()

    pltpu.make_async_remote_copy(
        src_ref=kvg_pair.at[c],
        dst_ref=kvg_pair.at[1 - c],
        send_sem=kvg_sem.at[0],
        recv_sem=kvg_sem.at[1],
        device_id={"head": sibling},
        device_id_type=MESH,
    ).wait_recv()

    def z_copy(i, core, to_z, head):
        return pltpu.make_async_remote_copy(
            src_ref=z_out.at[i, core],
            dst_ref=z_in.at[z],
            send_sem=z_send.at[i, core],
            recv_sem=z_recv.at[z],
            device_id={"group": to_z, "head": head},
            device_id_type=MESH,
        )

    for i, core in chunks:
        b = lax.rem(z + 1 + i, per_half)
        to_z = c * per_half + b
        at = pl.multiple_of(b * wide, wide)
        acc = q_term(y, b, core)
        acc = acc + dot_nt(kvg_pair[core], wkv_half[pl.ds(at, wide), :])
        for k in range(1, chips):
            part_copies[k, i, core].wait_recv()
            acc = acc + part_in[k - 1, i, core].astype(F32)
        z_out[i, core] = acc.astype(BF16)
        away = jnp.logical_or(to_z != z, core != c)

        @pl.when(away)
        def _():
            z_copy(i, core, to_z, y * CORES + core).start()

        @pl.when(jnp.logical_not(away))
        def _():
            z_in[z] = z_out[i, core]

    source_core = z // per_half
    result = None
    for source in range(groups):

        @pl.when(jnp.logical_or(source != z, source_core != c))
        def _():
            pltpu.make_async_remote_copy(
                src_ref=z_out.at[0, 0],
                dst_ref=z_in.at[source],
                send_sem=z_send.at[0, 0],
                recv_sem=z_recv.at[source],
                device_id={"head": sibling},
                device_id_type=MESH,
            ).wait_recv()

        term = z_in[source].astype(F32)
        result = term if result is None else result + term
    out_ref[...] = result.astype(BF16)

    for j in range(owners):

        @pl.when(CORES * j + my_half != h)
        def _():
            wkv_copy(j).wait_send()

    for copy in [w_copy, dq_copy, kvg_copy, *dkv_copies, *part_copies.values()]:
        copy.wait_send()
    for i, core in chunks:
        to_z = c * per_half + lax.rem(z + 1 + i, per_half)

        @pl.when(jnp.logical_or(to_z != z, core != c))
        def _():
            z_copy(i, core, to_z, y * CORES + core).wait_send()


def shards(groups, heads, *args):
    query, kv, q_weight, kv_weight = args[0], args[2], args[6], args[8]
    seq, size = query.shape
    model = q_weight.shape[0]
    chips = heads // CORES
    tokens = seq // heads
    wide = model // groups
    half = model // CORES
    per_half = groups // CORES
    owners = heads // CORES
    dma = pltpu.SemaphoreType.DMA
    vmem = pl.BlockSpec(memory_space=pltpu.VMEM)
    return pl.pallas_call(
        functools.partial(kernel, groups, heads),
        out_shape=(
            jax.ShapeDtypeStruct((tokens, wide), BF16),
            jax.ShapeDtypeStruct((tokens, 2 * size), BF16),
        ),
        in_specs=[vmem] * len(args),
        out_specs=(vmem, vmem),
        scratch_shapes=[
            pltpu.VMEM((half, 2 * size), BF16),
            pltpu.VMEM((half, size), BF16),
            pltpu.VMEM((half, 2 * size), BF16),
            pltpu.VMEM(kv_weight.shape, BF16),
            pltpu.VMEM((seq, 2 * size), BF16),
            pltpu.VMEM((seq, 2 * size), BF16),
            pltpu.VMEM((heads - 1, tokens, 2 * size), BF16),
            pltpu.VMEM((CORES, tokens, 2 * size), BF16),
            pltpu.VMEM((chips - 1, per_half, CORES, tokens, wide), BF16),
            pltpu.VMEM((chips - 1, per_half, CORES, tokens, wide), BF16),
            pltpu.VMEM((per_half, CORES, tokens, wide), BF16),
            pltpu.VMEM((groups, tokens, wide), BF16),
            pltpu.VMEM((seq, size), F32),
            pltpu.VMEM((seq, size), F32),
            dma((2,)),
            dma((owners,)),
            dma((owners,)),
            dma((2,)),
            dma((heads - 1,)),
            dma((heads - 1,)),
            dma((2,)),
            dma((chips - 1, per_half, CORES)),
            dma((chips - 1, per_half, CORES)),
            dma((per_half, CORES)),
            dma((groups,)),
        ],
        compiler_params=pltpu.CompilerParams(
            collective_id=0, has_side_effects=True, vmem_limit_bytes=48 * 1024 * 1024
        ),
    )(*args)


def solution(mesh):
    return jax.shard_map(
        functools.partial(shards, mesh.shape["group"], mesh.shape["head"]),
        mesh=mesh,
        in_specs=(
            P("dp", ("group", "head")),
            P(("group", "head"), "dp"),
            P("dp", "group"),
            P("group", "dp"),
            P("dp", ("group", "head")),
            P(("group", "head"), "dp"),
            P("dp", ("group", "head")),
            P("dp", ("group", "head")),
            P(("dp", "head"), "group"),
            P(("dp", "head"), "group"),
        ),
        out_specs=(P(("dp", "head"), "group"), P(("dp", "head"), "group")),
        check_vma=False,
    )
```

time: 89.1 us -> 43.1 us (0.48)
  the two profiles are of different devices: /device:TPU:0 before, /device:TPU:1 now
where the time goes in v1:
time: 43.1 us; the launch traced here: 42.6 us
  Pallas kernels  32.3 us (75%)
  local copies, waits for them, and re-layouts  9.61 us (22%)
  between operations  0.66 us (2%)
    pallas_call x1, Pallas kernels, shards(): pl.pallas_call(functools.partial(kernel, groups, heads), out_shape=(jax.S...  32.3 us
    unnamed x22, local copies, waits for them, and re-layouts  9.61 us

profile of v1, /device:TPU:1, one launch (start us, length us, event | category | flops | bytes accessed | tf_op | source)
XLA Modules:
  0.0 42.6 jit_solution(219691425163516996)
XLA Ops:
  0.6 0.0 copy-start
  0.6 1.0 %copy-done = bf16[2048,128]{1,0:T(8,128)(2,1)S(1)} copy-done((bf16[2048,128]{1,0:T(8,128)(2,1)S(1)}, bf16[2048,128]{1,0:T(8,128)(2,1)}, u32[]{:S(2)}) %copy-start) | copy-done | bytes 524312
  1.7 0.0 copy-start.1
  1.7 0.9 %copy-done.1 = bf16[512,256]{1,0:T(8,128)(2,1)S(1)} copy-done((bf16[512,256]{1,0:T(8,128)(2,1)S(1)}, bf16[512,256]{1,0:T(8,128)(2,1)}, u32[]{:S(2)}) %copy-start.1) | copy-done | bytes 262168
  2.6 0.0 copy-start.2
  2.6 0.9 %copy-done.2 = bf16[512,256]{1,0:T(8,128)(2,1)S(1)} copy-done((bf16[512,256]{1,0:T(8,128)(2,1)S(1)}, bf16[512,256]{1,0:T(8,128)(2,1)}, u32[]{:S(2)}) %copy-start.2) | copy-done | bytes 262168
  3.6 0.0 copy-start.3
  3.6 0.9 %copy-done.3 = bf16[512,128]{1,0:T(8,128)(2,1)S(1)} copy-done((bf16[512,128]{1,0:T(8,128)(2,1)S(1)}, bf16[512,128]{1,0:T(8,128)(2,1)}, u32[]{:S(2)}) %copy-start.3) | copy-done | bytes 131096
  4.5 0.0 copy-start.4
  4.5 0.9 %copy-done.4 = bf16[512,128]{1,0:T(8,128)(2,1)S(1)} copy-done((bf16[512,128]{1,0:T(8,128)(2,1)S(1)}, bf16[512,128]{1,0:T(8,128)(2,1)}, u32[]{:S(2)}) %copy-start.4) | copy-done | bytes 131096
  5.4 0.0 copy-start.5
  5.4 0.8 %copy-done.5 = s32[64,128]{1,0:T(8,128)S(1)} copy-done((s32[64,128]{1,0:T(8,128)S(1)}, s32[64,128]{1,0:T(8,128)}, u32[]{:S(2)}) %copy-start.5) | copy-done | bytes 32792
  6.1 0.0 copy-start.6
  6.1 0.7 %copy-done.6 = s32[8,512]{1,0:T(8,128)S(1)} copy-done((s32[8,512]{1,0:T(8,128)S(1)}, s32[8,512]{1,0:T(8,128)}, u32[]{:S(2)}) %copy-start.6) | copy-done | bytes 16408
  6.9 0.0 copy-start.7
  6.9 0.7 %copy-done.7 = s32[16,256]{1,0:T(8,128)S(1)} copy-done((s32[16,256]{1,0:T(8,128)S(1)}, s32[16,256]{1,0:T(8,128)}, u32[]{:S(2)}) %copy-start.7) | copy-done | bytes 16408
  7.6 0.0 copy-start.8
  7.6 0.7 %copy-done.8 = s32[4,512]{1,0:T(4,128)S(1)} copy-done((s32[4,512]{1,0:T(4,128)S(1)}, s32[4,512]{1,0:T(4,128)}, u32[]{:S(2)}) %copy-start.8) | copy-done | bytes 8216
  8.3 0.0 copy-start.9
  8.3 0.7 %copy-done.9 = s32[4,512]{1,0:T(4,128)S(1)} copy-done((s32[4,512]{1,0:T(4,128)S(1)}, s32[4,512]{1,0:T(4,128)}, u32[]{:S(2)}) %copy-start.9) | copy-done | bytes 8216
  9.0 32.3 %shard_map.113 = (bf16[128,512]{1,0:T(8,128)(2,1)S(1)}, bf16[128,256]{1,0:T(8,128)(2,1)S(1)}) custom-call(bf16[512,128]{1,0:T(8,128)(2,1)S(1)} %copy-done.3, s32[4,512]{1,0:T(4,128)S(1)} %copy-done.8, bf16[512,256]{1,0:T(8,128)(2,1)S(1)} %copy-done.1, s32[8,512]{1,0:T(8,128)S(1)} %copy-done.6, bf16[512,128]{1,0:T(8,128)(2,1)S(1)} %copy-done.4, ...), custom_call_target="tpu_custom_call" | custom-call | tf_op jit(solution)/shard_map/pallas_call | solution.py:355
  41.3 0.7 %copy.14 = bf16[128,512]{1,0:T(8,128)(2,1)} copy(bf16[128,512]{1,0:T(8,128)(2,1)S(1)} %get-tuple-element.4) | data formatting | bytes 262144
  41.9 0.6 %copy.15 = bf16[128,256]{1,0:T(8,128)(2,1)} copy(bf16[128,256]{1,0:T(8,128)(2,1)S(1)} %get-tuple-element.5) | data formatting | bytes 131072
Async XLA Ops:
  0.6 1.0 %copy-start = (bf16[2048,128]{1,0:T(8,128)(2,1)S(1)}, bf16[2048,128]{1,0:T(8,128)(2,1)}, u32[]{:S(2)}) copy-start(bf16[2048,128]{1,0:T(8,128)(2,1)} %wq_ref.1) | copy-start | bytes 1572868
  1.7 0.9 %copy-start.1 = (bf16[512,256]{1,0:T(8,128)(2,1)S(1)}, bf16[512,256]{1,0:T(8,128)(2,1)}, u32[]{:S(2)}) copy-start(bf16[512,256]{1,0:T(8,128)(2,1)} %kv_ref.1) | copy-start | bytes 786436
  2.6 0.9 %copy-start.2 = (bf16[512,256]{1,0:T(8,128)(2,1)S(1)}, bf16[512,256]{1,0:T(8,128)(2,1)}, u32[]{:S(2)}) copy-start(bf16[512,256]{1,0:T(8,128)(2,1)} %wkv_ref.1) | copy-start | bytes 786436
  3.6 0.9 %copy-start.3 = (bf16[512,128]{1,0:T(8,128)(2,1)S(1)}, bf16[512,128]{1,0:T(8,128)(2,1)}, u32[]{:S(2)}) copy-start(bf16[512,128]{1,0:T(8,128)(2,1)} %q_ref.1) | copy-start | bytes 393220
  4.5 0.9 %copy-start.4 = (bf16[512,128]{1,0:T(8,128)(2,1)S(1)}, bf16[512,128]{1,0:T(8,128)(2,1)}, u32[]{:S(2)}) copy-start(bf16[512,128]{1,0:T(8,128)(2,1)} %do_ref.1) | copy-start | bytes 393220
  5.4 0.8 %copy-start.5 = (s32[64,128]{1,0:T(8,128)S(1)}, s32[64,128]{1,0:T(8,128)}, u32[]{:S(2)}) copy-start(s32[64,128]{1,0:T(8,128)} %wqe_ref.1) | copy-start | bytes 98308
  6.1 0.7 %copy-start.6 = (s32[8,512]{1,0:T(8,128)S(1)}, s32[8,512]{1,0:T(8,128)}, u32[]{:S(2)}) copy-start(s32[8,512]{1,0:T(8,128)} %kve_ref.1) | copy-start | bytes 49156
  6.9 0.7 %copy-start.7 = (s32[16,256]{1,0:T(8,128)S(1)}, s32[16,256]{1,0:T(8,128)}, u32[]{:S(2)}) copy-start(s32[16,256]{1,0:T(8,128)} %wkve_ref.1) | copy-start | bytes 49156
  7.6 0.7 %copy-start.8 = (s32[4,512]{1,0:T(4,128)S(1)}, s32[4,512]{1,0:T(4,128)}, u32[]{:S(2)}) copy-start(s32[4,512]{1,0:T(4,128)} %qe_ref.1) | copy-start | bytes 24580
  8.3 0.7 %copy-start.9 = (s32[4,512]{1,0:T(4,128)S(1)}, s32[4,512]{1,0:T(4,128)}, u32[]{:S(2)}) copy-start(s32[4,512]{1,0:T(4,128)} %doe_ref.1) | copy-start | bytes 24580

commit v2 on v1

--- a/solution.py
+++ b/solution.py
@@ -12,6 +12,8 @@
 BF16 = jnp.bfloat16
 CORES = 2
 BLOCK = 32
+ARGS = 10
+LOAD_ORDER = (8, 9, 6, 7, 0, 1, 2, 3, 4, 5)
 
 
 def power_of_two(exponent):
@@ -45,44 +47,39 @@
 def kernel(
     groups,
     heads,
-    q_ref,
-    qe_ref,
-    kv_ref,
-    kve_ref,
-    do_ref,
-    doe_ref,
-    wq_ref,
-    wqe_ref,
-    wkv_ref,
-    wkve_ref,
-    out_ref,
-    kvg_ref,
-    wq_pair,
-    wq_out,
-    wkv_half,
-    wkv_out,
-    dq_pair,
-    dkv_out,
-    dkv_in,
-    kvg_pair,
-    part_out,
-    part_in,
-    z_out,
-    z_in,
-    dk_acc,
-    dv_acc,
-    w_sem,
-    wkv_send,
-    wkv_recv,
-    dq_sem,
-    dkv_send,
-    dkv_recv,
-    kvg_sem,
-    part_send,
-    part_recv,
-    z_send,
-    z_recv,
+    *refs,
 ):
+    sources, (out_ref, kvg_ref) = refs[:ARGS], refs[ARGS : ARGS + 2]
+    held = refs[ARGS + 2 : 2 * ARGS + 2]
+    q_ref, qe_ref, kv_ref, kve_ref, do_ref, doe_ref, wq_ref, wqe_ref, wkv_ref, wkve_ref = held
+    (
+        load_sem,
+        wq_pair,
+        wq_out,
+        wkv_half,
+        wkv_out,
+        dq_pair,
+        dkv_out,
+        dkv_in,
+        kvg_pair,
+        part_out,
+        part_in,
+        z_out,
+        z_in,
+        dk_acc,
+        dv_acc,
+        w_sem,
+        wkv_send,
+        wkv_recv,
+        dq_sem,
+        dkv_send,
+        dkv_recv,
+        kvg_sem,
+        part_send,
+        part_recv,
+        z_send,
+        z_recv,
+    ) = refs[2 * ARGS + 2 :]
     seq, size = q_ref.shape
     model = wq_ref.shape[0]
     chips = heads // CORES
@@ -99,6 +96,13 @@
     y = h // CORES
     c = lax.rem(h, CORES)
     sibling = y * CORES + (1 - c)
+
+    loads = [
+        pltpu.make_async_copy(source, held[at], load_sem.at[at])
+        for at, source in enumerate(sources)
+    ]
+    for at in LOAD_ORDER:
+        loads[at].start()
 
     barrier = pltpu.get_barrier_semaphore()
     for k in range(1, heads):
@@ -121,6 +125,8 @@
             wq_ref[pl.ds(first, half), :], wqe_ref[pl.ds(first_e, half // BLOCK), :]
         )
 
+    for at in LOAD_ORDER[:4]:
+        loads[at].wait()
     wq_out[...] = weight_rows(1 - c)
     wkv_out[...] = dequant_cols(wkv_ref[...], wkve_ref[...])
     pl.semaphore_wait(barrier, heads - 1 + CORES * (groups - 1))
@@ -159,6 +165,8 @@
     def _():
         wkv_half[pl.ds(my_slot, rows), :] = wkv_out[...]
 
+    for at in LOAD_ORDER[4:]:
+        loads[at].wait()
     query = dequant_rows(q_ref[...], qe_ref[...])
     kv = dequant_rows(kv_ref[...], kve_ref[...])
     grad = dequant_rows(do_ref[...], doe_ref[...])
@@ -358,9 +366,11 @@
             jax.ShapeDtypeStruct((tokens, wide), BF16),
             jax.ShapeDtypeStruct((tokens, 2 * size), BF16),
         ),
-        in_specs=[vmem] * len(args),
+        in_specs=[pl.BlockSpec(memory_space=pltpu.HBM)] * ARGS,
         out_specs=(vmem, vmem),
-        scratch_shapes=[
+        scratch_shapes=[pltpu.VMEM(arg.shape, arg.dtype) for arg in args]
+        + [
+            dma((ARGS,)),
             pltpu.VMEM((half, 2 * size), BF16),
             pltpu.VMEM((half, size), BF16),
             pltpu.VMEM((half, 2 * size), BF16),
@@ -388,7 +398,7 @@
             dma((groups,)),
         ],
         compiler_params=pltpu.CompilerParams(
-            collective_id=0, has_side_effects=True, vmem_limit_bytes=48 * 1024 * 1024
+            collective_id=0, has_side_effects=True, vmem_limit_bytes=63 * 1024 * 1024
         ),
     )(*args)
 

time: 43.1 us -> 36.3 us (0.84)
  local copies, waits for them, and re-layouts: 9.61 us -> 2.23 us
  Pallas kernels: 32.3 us -> 33.3 us
    unnamed x22 -> x4, local copies, waits for them, and re-layouts: 9.61 us -> 2.23 us
    pallas_call x1, Pallas kernels: 32.3 us -> 33.3 us  [shards(): pl.pallas_call(functools.partial(kernel, groups, heads), out_shape=(jax.S...]
where the time goes in v2:
time: 36.3 us; the launch traced here: 36.2 us
  Pallas kernels  33.3 us (92%)
  local copies, waits for them, and re-layouts  2.23 us (6%)
  between operations  0.65 us (2%)
    pallas_call x1, Pallas kernels, shards(): pl.pallas_call(functools.partial(kernel, groups, heads), out_shape=(jax.S...  33.3 us
    unnamed x4, local copies, waits for them, and re-layouts  2.23 us

profile of v2, /device:TPU:1, one launch (start us, length us, event | category | flops | bytes accessed | tf_op | source)
XLA Modules:
  0.0 36.2 jit_solution(15431190983231233939)
XLA Ops:
  0.6 33.3 %shard_map.113 = (bf16[128,512]{1,0:T(8,128)(2,1)}, bf16[128,256]{1,0:T(8,128)(2,1)}) custom-call(bf16[512,128]{1,0:T(8,128)(2,1)} %refs_0_.1, s32[4,512]{1,0:T(4,128)} %refs_1_.1, bf16[512,256]{1,0:T(8,128)(2,1)} %refs_2_.1, s32[8,512]{1,0:T(8,128)} %refs_3_.1, bf16[512,128]{1,0:T(8,128)(2,1)} %refs_4_.1, s32[4,512]{1,0:T(4,128)} %refs_5_.1, ...), custom_call_target="tpu_custom_call" | custom-call | tf_op jit(solution)/shard_map/pallas_call | solution.py:363
  33.9 0.0 copy-start
  34.0 1.6 %copy.14 = bf16[128,512]{1,0:T(8,128)(2,1)} copy(bf16[128,512]{1,0:T(8,128)(2,1)} %get-tuple-element.4) | data formatting | bytes 262144
  35.6 0.0 copy-done
  35.6 0.6 %copy.15 = bf16[128,256]{1,0:T(8,128)(2,1)} copy(bf16[128,256]{1,0:T(8,128)(2,1)S(1)} %copy-done) | data formatting | bytes 131072
Async XLA Ops:
  33.9 1.6 %copy-start = (bf16[128,256]{1,0:T(8,128)(2,1)S(1)}, bf16[128,256]{1,0:T(8,128)(2,1)}, u32[]{:S(2)}) copy-start(bf16[128,256]{1,0:T(8,128)(2,1)} %get-tuple-element.5) | copy-start | bytes 196612

commit v3 on v2

--- a/solution.py
+++ b/solution.py
@@ -13,6 +13,7 @@
 CORES = 2
 BLOCK = 32
 ARGS = 10
+PIECES = 2
 LOAD_ORDER = (8, 9, 6, 7, 0, 1, 2, 3, 4, 5)
 
 
@@ -60,6 +61,8 @@
         wkv_out,
         dq_pair,
         dkv_out,
+        dkv_near,
+        dkv_sum,
         dkv_in,
         kvg_pair,
         part_out,
@@ -72,6 +75,8 @@
         wkv_send,
         wkv_recv,
         dq_sem,
+        near_send,
+        near_recv,
         dkv_send,
         dkv_recv,
         kvg_sem,
@@ -87,6 +92,7 @@
     wide = model // groups
     half = model // CORES
     per_half = groups // CORES
+    piece = tokens // PIECES
     rows = wkv_ref.shape[0]
     owners = heads // CORES
     scale = 1.0 / size**0.5
@@ -125,9 +131,8 @@
             wq_ref[pl.ds(first, half), :], wqe_ref[pl.ds(first_e, half // BLOCK), :]
         )
 
-    for at in LOAD_ORDER[:4]:
+    for at in LOAD_ORDER[:2]:
         loads[at].wait()
-    wq_out[...] = weight_rows(1 - c)
     wkv_out[...] = dequant_cols(wkv_ref[...], wkve_ref[...])
     pl.semaphore_wait(barrier, heads - 1 + CORES * (groups - 1))
 
@@ -150,6 +155,9 @@
         def _():
             wkv_copy(j).start()
 
+    for at in LOAD_ORDER[2:4]:
+        loads[at].wait()
+    wq_out[...] = weight_rows(1 - c)
     w_copy = pltpu.make_async_remote_copy(
         src_ref=wq_out,
         dst_ref=wq_pair.at[:, size:],
@@ -206,47 +214,72 @@
     dq_copy.start()
     dkv_out[:, :size] = dk_acc[...].astype(BF16)
     dkv_out[:, size:] = dv_acc[...].astype(BF16)
+
+    def chip_rows(chip, core):
+        return pl.ds(pl.multiple_of((chip * CORES + core) * tokens, tokens), tokens)
+
+    near_copies = []
+    for k in [*range(1, chips), 0]:
+        copy = pltpu.make_async_remote_copy(
+            src_ref=dkv_out.at[chip_rows(lax.rem(y + k, chips), 1 - c)],
+            dst_ref=dkv_near.at[k],
+            send_sem=near_send.at[k],
+            recv_sem=near_recv.at[k],
+            device_id={"head": sibling},
+            device_id_type=MESH,
+        )
+        copy.start()
+        near_copies.append(copy)
     dkv_copies = []
-    for k in range(1, heads):
-        to = lax.rem(h + k, heads)
+    for k in range(1, chips):
+        to = lax.rem(y + k, chips)
+        near_copies[k - 1].wait_recv()
+        both = dkv_out[chip_rows(to, c), :].astype(F32) + dkv_near[k].astype(F32)
+        dkv_sum[k - 1] = both.astype(BF16)
         copy = pltpu.make_async_remote_copy(
-            src_ref=dkv_out.at[pl.ds(pl.multiple_of(to * tokens, tokens), tokens)],
+            src_ref=dkv_sum.at[k - 1],
             dst_ref=dkv_in.at[k - 1],
             send_sem=dkv_send.at[k - 1],
             recv_sem=dkv_recv.at[k - 1],
-            device_id={"head": to},
+            device_id={"head": to * CORES + c},
             device_id_type=MESH,
         )
         copy.start()
         dkv_copies.append(copy)
 
-    def q_term(chip, b, core):
-        first = pl.multiple_of((chip * CORES + core) * tokens, tokens)
+    def q_term(chip, b, e):
+        first = pl.multiple_of(chip * CORES * tokens + e * piece, piece)
         at = pl.multiple_of(b * wide, wide)
-        return dot_nt(dq_pair[pl.ds(first, tokens), :], wq_pair[pl.ds(at, wide), :])
+        return dot_nt(dq_pair[pl.ds(first, piece), :], wq_pair[pl.ds(at, wide), :])
 
     w_copy.wait_recv()
     dq_copy.wait_recv()
-    chunks = [(i, core) for i in range(per_half) for core in range(CORES)]
+    chunks = [
+        (i, core * PIECES + p)
+        for i in range(per_half)
+        for p in range(PIECES)
+        for core in range(CORES)
+    ]
     part_copies = {}
-    for i, core in chunks:
+    for i, e in chunks:
         b = lax.rem(z + 1 + i, per_half)
         for k in range(1, chips):
             to = lax.rem(y + k, chips)
-            part_out[k - 1, i, core] = q_term(to, b, core).astype(BF16)
+            part_out[k - 1, i, e] = q_term(to, b, e).astype(BF16)
             copy = pltpu.make_async_remote_copy(
-                src_ref=part_out.at[k - 1, i, core],
-                dst_ref=part_in.at[k - 1, i, core],
-                send_sem=part_send.at[k - 1, i, core],
-                recv_sem=part_recv.at[k - 1, i, core],
+                src_ref=part_out.at[k - 1, i, e],
+                dst_ref=part_in.at[k - 1, i, e],
+                send_sem=part_send.at[k - 1, i, e],
+                recv_sem=part_recv.at[k - 1, i, e],
                 device_id={"head": to * CORES + c},
                 device_id_type=MESH,
             )
             copy.start()
-            part_copies[k, i, core] = copy
-
-    total = dkv_out[pl.ds(pl.multiple_of(h * tokens, tokens), tokens), :].astype(F32)
-    for k in range(1, heads):
+            part_copies[k, i, e] = copy
+
+    near_copies[-1].wait_recv()
+    total = dkv_out[chip_rows(y, c), :].astype(F32) + dkv_near[0].astype(F32)
+    for k in range(1, chips):
         dkv_copies[k - 1].wait_recv()
         total = total + dkv_in[k - 1].astype(F32)
     kvg = total.astype(BF16)
@@ -283,54 +316,56 @@
         device_id_type=MESH,
     ).wait_recv()
 
-    def z_copy(i, core, to_z, head):
+    def z_copy(i, e, to_z):
         return pltpu.make_async_remote_copy(
-            src_ref=z_out.at[i, core],
-            dst_ref=z_in.at[z],
-            send_sem=z_send.at[i, core],
-            recv_sem=z_recv.at[z],
-            device_id={"group": to_z, "head": head},
+            src_ref=z_out.at[i, e],
+            dst_ref=z_in.at[z, e % PIECES],
+            send_sem=z_send.at[i, e],
+            recv_sem=z_recv.at[z, e % PIECES],
+            device_id={"group": to_z, "head": y * CORES + e // PIECES},
             device_id_type=MESH,
         )
 
-    for i, core in chunks:
+    for i, e in chunks:
         b = lax.rem(z + 1 + i, per_half)
         to_z = c * per_half + b
         at = pl.multiple_of(b * wide, wide)
-        acc = q_term(y, b, core)
-        acc = acc + dot_nt(kvg_pair[core], wkv_half[pl.ds(at, wide), :])
+        acc = q_term(y, b, e)
+        kvg_piece = kvg_pair[e // PIECES, pl.ds(e % PIECES * piece, piece), :]
+        acc = acc + dot_nt(kvg_piece, wkv_half[pl.ds(at, wide), :])
         for k in range(1, chips):
-            part_copies[k, i, core].wait_recv()
-            acc = acc + part_in[k - 1, i, core].astype(F32)
-        z_out[i, core] = acc.astype(BF16)
-        away = jnp.logical_or(to_z != z, core != c)
+            part_copies[k, i, e].wait_recv()
+            acc = acc + part_in[k - 1, i, e].astype(F32)
+        z_out[i, e] = acc.astype(BF16)
+        away = jnp.logical_or(to_z != z, e // PIECES != c)
 
         @pl.when(away)
         def _():
-            z_copy(i, core, to_z, y * CORES + core).start()
+            z_copy(i, e, to_z).start()
 
         @pl.when(jnp.logical_not(away))
         def _():
-            z_in[z] = z_out[i, core]
+            z_in[z, e % PIECES] = z_out[i, e]
 
     source_core = z // per_half
-    result = None
-    for source in range(groups):
-
-        @pl.when(jnp.logical_or(source != z, source_core != c))
-        def _():
-            pltpu.make_async_remote_copy(
-                src_ref=z_out.at[0, 0],
-                dst_ref=z_in.at[source],
-                send_sem=z_send.at[0, 0],
-                recv_sem=z_recv.at[source],
-                device_id={"head": sibling},
-                device_id_type=MESH,
-            ).wait_recv()
-
-        term = z_in[source].astype(F32)
-        result = term if result is None else result + term
-    out_ref[...] = result.astype(BF16)
+    for p in range(PIECES):
+        result = None
+        for source in range(groups):
+
+            @pl.when(jnp.logical_or(source != z, source_core != c))
+            def _():
+                pltpu.make_async_remote_copy(
+                    src_ref=z_out.at[0, 0],
+                    dst_ref=z_in.at[source, p],
+                    send_sem=z_send.at[0, 0],
+                    recv_sem=z_recv.at[source, p],
+                    device_id={"head": sibling},
+                    device_id_type=MESH,
+                ).wait_recv()
+
+            term = z_in[source, p].astype(F32)
+            result = term if result is None else result + term
+        out_ref[p * piece : (p + 1) * piece, :] = result.astype(BF16)
 
     for j in range(owners):
 
@@ -338,14 +373,14 @@
         def _():
             wkv_copy(j).wait_send()
 
-    for copy in [w_copy, dq_copy, kvg_copy, *dkv_copies, *part_copies.values()]:
+    for copy in [w_copy, dq_copy, kvg_copy, *near_copies, *dkv_copies, *part_copies.values()]:
         copy.wait_send()
-    for i, core in chunks:
+    for i, e in chunks:
         to_z = c * per_half + lax.rem(z + 1 + i, per_half)
 
-        @pl.when(jnp.logical_or(to_z != z, core != c))
-        def _():
-            z_copy(i, core, to_z, y * CORES + core).wait_send()
+        @pl.when(jnp.logical_or(to_z != z, e // PIECES != c))
+        def _():
+            z_copy(i, e, to_z).wait_send()
 
 
 def shards(groups, heads, *args):
@@ -354,6 +389,7 @@
     model = q_weight.shape[0]
     chips = heads // CORES
     tokens = seq // heads
+    piece = tokens // PIECES
     wide = model // groups
     half = model // CORES
     per_half = groups // CORES
@@ -377,25 +413,29 @@
             pltpu.VMEM(kv_weight.shape, BF16),
             pltpu.VMEM((seq, 2 * size), BF16),
             pltpu.VMEM((seq, 2 * size), BF16),
-            pltpu.VMEM((heads - 1, tokens, 2 * size), BF16),
+            pltpu.VMEM((chips, tokens, 2 * size), BF16),
+            pltpu.VMEM((chips - 1, tokens, 2 * size), BF16),
+            pltpu.VMEM((chips - 1, tokens, 2 * size), BF16),
             pltpu.VMEM((CORES, tokens, 2 * size), BF16),
-            pltpu.VMEM((chips - 1, per_half, CORES, tokens, wide), BF16),
-            pltpu.VMEM((chips - 1, per_half, CORES, tokens, wide), BF16),
-            pltpu.VMEM((per_half, CORES, tokens, wide), BF16),
-            pltpu.VMEM((groups, tokens, wide), BF16),
+            pltpu.VMEM((chips - 1, per_half, CORES * PIECES, piece, wide), BF16),
+            pltpu.VMEM((chips - 1, per_half, CORES * PIECES, piece, wide), BF16),
+            pltpu.VMEM((per_half, CORES * PIECES, piece, wide), BF16),
+            pltpu.VMEM((groups, PIECES, piece, wide), BF16),
             pltpu.VMEM((seq, size), F32),
             pltpu.VMEM((seq, size), F32),
             dma((2,)),
             dma((owners,)),
             dma((owners,)),
             dma((2,)),
-            dma((heads - 1,)),
-            dma((heads - 1,)),
+            dma((chips,)),
+            dma((chips,)),
+            dma((chips - 1,)),
+            dma((chips - 1,)),
             dma((2,)),
-            dma((chips - 1, per_half, CORES)),
-            dma((chips - 1, per_half, CORES)),
-            dma((per_half, CORES)),
-            dma((groups,)),
+            dma((chips - 1, per_half, CORES * PIECES)),
+            dma((chips - 1, per_half, CORES * PIECES)),
+            dma((per_half, CORES * PIECES)),
+            dma((groups, PIECES)),
         ],
         compiler_params=pltpu.CompilerParams(
             collective_id=0, has_side_effects=True, vmem_limit_bytes=63 * 1024 * 1024

time: 36.3 us -> 33.8 us (0.931)
  Pallas kernels: 33.3 us -> 30.8 us
    pallas_call x1, Pallas kernels: 33.3 us -> 30.8 us  [shards(): pl.pallas_call(functools.partial(kernel, groups, heads), out_shape=(jax.S...]
where the time goes in v3:
time: 33.8 us; the launch traced here: 33.7 us
  Pallas kernels  30.8 us (91%)
  local copies, waits for them, and re-layouts  2.23 us (7%)
  between operations  0.65 us (2%)
    pallas_call x1, Pallas kernels, shards(): pl.pallas_call(functools.partial(kernel, groups, heads), out_shape=(jax.S...  30.8 us
    unnamed x4, local copies, waits for them, and re-layouts  2.23 us

profile of v3, /device:TPU:1, one launch (start us, length us, event | category | flops | bytes accessed | tf_op | source)
XLA Modules:
  0.0 33.7 jit_solution(15887512558756091036)
XLA Ops:
  0.6 30.8 %shard_map.113 = (bf16[128,512]{1,0:T(8,128)(2,1)}, bf16[128,256]{1,0:T(8,128)(2,1)}) custom-call(bf16[512,128]{1,0:T(8,128)(2,1)} %refs_0_.1, s32[4,512]{1,0:T(4,128)} %refs_1_.1, bf16[512,256]{1,0:T(8,128)(2,1)} %refs_2_.1, s32[8,512]{1,0:T(8,128)} %refs_3_.1, bf16[512,128]{1,0:T(8,128)(2,1)} %refs_4_.1, s32[4,512]{1,0:T(4,128)} %refs_5_.1, ...), custom_call_target="tpu_custom_call" | custom-call | tf_op jit(solution)/shard_map/pallas_call | solution.py:399
  31.4 0.0 copy-start
  31.4 1.6 %copy.14 = bf16[128,512]{1,0:T(8,128)(2,1)} copy(bf16[128,512]{1,0:T(8,128)(2,1)} %get-tuple-element.4) | data formatting | bytes 262144
  33.0 0.0 copy-done
  33.0 0.6 %copy.15 = bf16[128,256]{1,0:T(8,128)(2,1)} copy(bf16[128,256]{1,0:T(8,128)(2,1)S(1)} %copy-done) | data formatting | bytes 131072
Async XLA Ops:
  31.4 1.6 %copy-start = (bf16[128,256]{1,0:T(8,128)(2,1)S(1)}, bf16[128,256]{1,0:T(8,128)(2,1)}, u32[]{:S(2)}) copy-start(bf16[128,256]{1,0:T(8,128)(2,1)} %get-tuple-element.5) | copy-start | bytes 196612

commit v4 on v3

--- a/solution.py
+++ b/solution.py
@@ -14,6 +14,7 @@
 BLOCK = 32
 ARGS = 10
 PIECES = 2
+AHEAD = 4
 LOAD_ORDER = (8, 9, 6, 7, 0, 1, 2, 3, 4, 5)
 
 
@@ -261,7 +262,8 @@
         for core in range(CORES)
     ]
     part_copies = {}
-    for i, e in chunks:
+
+    def send_part(i, e):
         b = lax.rem(z + 1 + i, per_half)
         for k in range(1, chips):
             to = lax.rem(y + k, chips)
@@ -276,6 +278,9 @@
             )
             copy.start()
             part_copies[k, i, e] = copy
+
+    for i, e in chunks[:AHEAD]:
+        send_part(i, e)
 
     near_copies[-1].wait_recv()
     total = dkv_out[chip_rows(y, c), :].astype(F32) + dkv_near[0].astype(F32)
@@ -326,7 +331,7 @@
             device_id_type=MESH,
         )
 
-    for i, e in chunks:
+    for n, (i, e) in enumerate(chunks):
         b = lax.rem(z + 1 + i, per_half)
         to_z = c * per_half + b
         at = pl.multiple_of(b * wide, wide)
@@ -347,6 +352,11 @@
         def _():
             z_in[z, e % PIECES] = z_out[i, e]
 
+        if n + AHEAD < len(chunks):
+            for k in range(1, chips):
+                part_copies[k, i, e].wait_send()
+            send_part(*chunks[n + AHEAD])
+
     source_core = z // per_half
     for p in range(PIECES):
         result = None
@@ -373,8 +383,11 @@
         def _():
             wkv_copy(j).wait_send()
 
-    for copy in [w_copy, dq_copy, kvg_copy, *near_copies, *dkv_copies, *part_copies.values()]:
+    for copy in [w_copy, dq_copy, kvg_copy, *near_copies, *dkv_copies]:
         copy.wait_send()
+    for i, e in chunks[-AHEAD:]:
+        for k in range(1, chips):
+            part_copies[k, i, e].wait_send()
     for i, e in chunks:
         to_z = c * per_half + lax.rem(z + 1 + i, per_half)
 
@@ -399,8 +412,8 @@
     return pl.pallas_call(
         functools.partial(kernel, groups, heads),
         out_shape=(
-            jax.ShapeDtypeStruct((tokens, wide), BF16),
-            jax.ShapeDtypeStruct((tokens, 2 * size), BF16),
+            pltpu.VMEM((tokens, wide), BF16),
+            pltpu.VMEM((tokens, 2 * size), BF16),
         ),
         in_specs=[pl.BlockSpec(memory_space=pltpu.HBM)] * ARGS,
         out_specs=(vmem, vmem),
@@ -438,7 +451,7 @@
             dma((groups, PIECES)),
         ],
         compiler_params=pltpu.CompilerParams(
-            collective_id=0, has_side_effects=True, vmem_limit_bytes=63 * 1024 * 1024
+            collective_id=0, has_side_effects=True, vmem_limit_bytes=55 * 1024 * 1024
         ),
     )(*args)
 

time: 33.8 us -> 32.2 us (0.953)
  local copies, waits for them, and re-layouts: 2.23 us -> 1.29 us
  Pallas kernels: 30.8 us -> 30.1 us
    unnamed x4 -> x2, local copies, waits for them, and re-layouts: 2.23 us -> 1.29 us
    pallas_call x1, Pallas kernels: 30.8 us -> 30.1 us  [shards(): pl.pallas_call(functools.partial(kernel, groups, heads), out_shape=(pltpu...]
where the time goes in v4:
time: 32.2 us; the launch traced here: 32 us
  Pallas kernels  30.1 us (93%)
  local copies, waits for them, and re-layouts  1.29 us (4%)
  between operations  0.64 us (2%)
    pallas_call x1, Pallas kernels, shards(): pl.pallas_call(functools.partial(kernel, groups, heads), out_shape=(pltpu...  30.1 us
    unnamed x2, local copies, waits for them, and re-layouts  1.29 us

profile of v4, /device:TPU:1, one launch (start us, length us, event | category | flops | bytes accessed | tf_op | source)
XLA Modules:
  0.0 32.0 jit_solution(14666366910195972244)
XLA Ops:
  0.6 30.1 %shard_map.113 = (bf16[128,512]{1,0:T(8,128)(2,1)S(1)}, bf16[128,256]{1,0:T(8,128)(2,1)S(1)}) custom-call(bf16[512,128]{1,0:T(8,128)(2,1)} %refs_0_.1, s32[4,512]{1,0:T(4,128)} %refs_1_.1, bf16[512,256]{1,0:T(8,128)(2,1)} %refs_2_.1, s32[8,512]{1,0:T(8,128)} %refs_3_.1, bf16[512,128]{1,0:T(8,128)(2,1)} %refs_4_.1, s32[4,512]{1,0:T(4,128)} %refs_5_.1, ...), custom_call_target="tpu_custom_call" | custom-call | tf_op jit(solution)/shard_map/pallas_call | solution.py:412
  30.7 0.7 %copy.14 = bf16[128,512]{1,0:T(8,128)(2,1)} copy(bf16[128,512]{1,0:T(8,128)(2,1)S(1)} %get-tuple-element.2) | data formatting | bytes 262144
  31.4 0.6 %copy.15 = bf16[128,256]{1,0:T(8,128)(2,1)} copy(bf16[128,256]{1,0:T(8,128)(2,1)S(1)} %get-tuple-element.3) | data formatting | bytes 131072

commit v5 on v4

--- a/solution.py
+++ b/solution.py
@@ -75,7 +75,8 @@
         w_sem,
         wkv_send,
         wkv_recv,
-        dq_sem,
+        dq_send,
+        dq_recv,
         near_send,
         near_recv,
         dkv_send,
@@ -176,43 +177,45 @@
 
     for at in LOAD_ORDER[4:]:
         loads[at].wait()
-    query = dequant_rows(q_ref[...], qe_ref[...])
     kv = dequant_rows(kv_ref[...], kve_ref[...])
-    grad = dequant_rows(do_ref[...], doe_ref[...])
     keys, values = kv[:, :size], kv[:, size:]
-    block = min(256, seq)
-    for index in reversed(range(seq // block)):
-        first, upper = index * block, (index + 1) * block
-        q_block, do_block = query[first:upper], grad[first:upper]
-        scores = dot_nt(keys[:upper], q_block)
-        key_at = lax.broadcasted_iota(jnp.int32, (upper, block), 0)
-        query_at = first + lax.broadcasted_iota(jnp.int32, (upper, block), 1)
-        scores = jnp.where(key_at <= query_at, scores, -jnp.inf)
+    block = CORES * tokens
+    key_at = lax.broadcasted_iota(jnp.int32, (seq, block), 0)
+    query_at = lax.broadcasted_iota(jnp.int32, (seq, block), 1)
+    dq_copies = []
+    for k in [*range(1, chips), 0]:
+        first = pl.multiple_of(lax.rem(y + k, chips) * block, block)
+        at = pl.ds(first, block)
+        q_block = dequant_rows(q_ref[at, :], qe_ref[:, at])
+        do_block = dequant_rows(do_ref[at, :], doe_ref[:, at])
+        scores = dot_nt(keys, q_block)
+        scores = jnp.where(key_at <= first + query_at, scores, -jnp.inf)
         expd = jnp.exp((scores - jnp.max(scores, axis=0, keepdims=True)) * scale)
         probs = expd * (1.0 / jnp.sum(expd, axis=0, keepdims=True))
         probs_b = probs.astype(BF16)
-        dprob = dot_nt(values[:upper], do_block)
+        dprob = dot_nt(values, do_block)
         delta = jnp.sum(probs_b.astype(F32) * dprob, axis=0, keepdims=True)
         dscore = (probs * (dprob - delta) * scale).astype(BF16)
-        dq_pair[first:upper, :size] = dot_tn(dscore, keys[:upper]).astype(BF16)
+        dq_pair[at, :size] = dot_tn(dscore, keys).astype(BF16)
+        copy = pltpu.make_async_remote_copy(
+            src_ref=dq_pair.at[at, pl.ds(0, size)],
+            dst_ref=dq_pair.at[at, pl.ds(size, size)],
+            send_sem=dq_send.at[k],
+            recv_sem=dq_recv.at[k],
+            device_id={"head": sibling},
+            device_id_type=MESH,
+        )
+        copy.start()
+        dq_copies.append(copy)
         dk = jnp.dot(dscore, q_block, preferred_element_type=F32)
         dv = jnp.dot(probs_b, do_block, preferred_element_type=F32)
-        if upper == seq:
+        if len(dq_copies) == 1:
             dk_acc[...] = dk
             dv_acc[...] = dv
         else:
-            dk_acc[:upper, :] += dk
-            dv_acc[:upper, :] += dv
-
-    dq_copy = pltpu.make_async_remote_copy(
-        src_ref=dq_pair.at[:, :size],
-        dst_ref=dq_pair.at[:, size:],
-        send_sem=dq_sem.at[0],
-        recv_sem=dq_sem.at[1],
-        device_id={"head": sibling},
-        device_id_type=MESH,
-    )
-    dq_copy.start()
+            dk_acc[...] += dk
+            dv_acc[...] += dv
+
     dkv_out[:, :size] = dk_acc[...].astype(BF16)
     dkv_out[:, size:] = dv_acc[...].astype(BF16)
 
@@ -231,30 +234,14 @@
         )
         copy.start()
         near_copies.append(copy)
-    dkv_copies = []
-    for k in range(1, chips):
-        to = lax.rem(y + k, chips)
-        near_copies[k - 1].wait_recv()
-        both = dkv_out[chip_rows(to, c), :].astype(F32) + dkv_near[k].astype(F32)
-        dkv_sum[k - 1] = both.astype(BF16)
-        copy = pltpu.make_async_remote_copy(
-            src_ref=dkv_sum.at[k - 1],
-            dst_ref=dkv_in.at[k - 1],
-            send_sem=dkv_send.at[k - 1],
-            recv_sem=dkv_recv.at[k - 1],
-            device_id={"head": to * CORES + c},
-            device_id_type=MESH,
-        )
-        copy.start()
-        dkv_copies.append(copy)
-
     def q_term(chip, b, e):
         first = pl.multiple_of(chip * CORES * tokens + e * piece, piece)
         at = pl.multiple_of(b * wide, wide)
         return dot_nt(dq_pair[pl.ds(first, piece), :], wq_pair[pl.ds(at, wide), :])
 
     w_copy.wait_recv()
-    dq_copy.wait_recv()
+    for copy in dq_copies[:-1]:
+        copy.wait_recv()
     chunks = [
         (i, core * PIECES + p)
         for i in range(per_half)
@@ -279,8 +266,29 @@
             copy.start()
             part_copies[k, i, e] = copy
 
-    for i, e in chunks[:AHEAD]:
+    for i, e in chunks[: AHEAD // 2]:
         send_part(i, e)
+
+    dkv_copies = []
+    for k in range(1, chips):
+        to = lax.rem(y + k, chips)
+        near_copies[k - 1].wait_recv()
+        both = dkv_out[chip_rows(to, c), :].astype(F32) + dkv_near[k].astype(F32)
+        dkv_sum[k - 1] = both.astype(BF16)
+        copy = pltpu.make_async_remote_copy(
+            src_ref=dkv_sum.at[k - 1],
+            dst_ref=dkv_in.at[k - 1],
+            send_sem=dkv_send.at[k - 1],
+            recv_sem=dkv_recv.at[k - 1],
+            device_id={"head": to * CORES + c},
+            device_id_type=MESH,
+        )
+        copy.start()
+        dkv_copies.append(copy)
+
+    for i, e in chunks[AHEAD // 2 : AHEAD]:
+        send_part(i, e)
+    dq_copies[-1].wait_recv()
 
     near_copies[-1].wait_recv()
     total = dkv_out[chip_rows(y, c), :].astype(F32) + dkv_near[0].astype(F32)
@@ -383,7 +391,7 @@
         def _():
             wkv_copy(j).wait_send()
 
-    for copy in [w_copy, dq_copy, kvg_copy, *near_copies, *dkv_copies]:
+    for copy in [w_copy, *dq_copies, kvg_copy, *near_copies, *dkv_copies]:
         copy.wait_send()
     for i, e in chunks[-AHEAD:]:
         for k in range(1, chips):
@@ -439,7 +447,8 @@
             dma((2,)),
             dma((owners,)),
             dma((owners,)),
-            dma((2,)),
+            dma((chips,)),
+            dma((chips,)),
             dma((chips,)),
             dma((chips,)),
             dma((chips - 1,)),

time: 32.2 us -> 33.7 us (1.047)
  Pallas kernels: 30.1 us -> 31.6 us
    pallas_call x1, Pallas kernels: 30.1 us -> 31.6 us  [shards(): pl.pallas_call(functools.partial(kernel, groups, heads), out_shape=(pltpu...]
where the time goes in v5:
time: 33.7 us; the launch traced here: 33.5 us
  Pallas kernels  31.6 us (94%)
  local copies, waits for them, and re-layouts  1.29 us (4%)
  between operations  0.64 us (2%)
    pallas_call x1, Pallas kernels, shards(): pl.pallas_call(functools.partial(kernel, groups, heads), out_shape=(pltpu...  31.6 us
    unnamed x2, local copies, waits for them, and re-layouts  1.29 us

profile of v5, /device:TPU:1, one launch (start us, length us, event | category | flops | bytes accessed | tf_op | source)
XLA Modules:
  0.0 33.5 jit_solution(4072226492557773885)
XLA Ops:
  0.6 31.6 %shard_map.113 = (bf16[128,512]{1,0:T(8,128)(2,1)S(1)}, bf16[128,256]{1,0:T(8,128)(2,1)S(1)}) custom-call(bf16[512,128]{1,0:T(8,128)(2,1)} %refs_0_.1, s32[4,512]{1,0:T(4,128)} %refs_1_.1, bf16[512,256]{1,0:T(8,128)(2,1)} %refs_2_.1, s32[8,512]{1,0:T(8,128)} %refs_3_.1, bf16[512,128]{1,0:T(8,128)(2,1)} %refs_4_.1, s32[4,512]{1,0:T(4,128)} %refs_5_.1, ...), custom_call_target="tpu_custom_call" | custom-call | tf_op jit(solution)/shard_map/pallas_call | solution.py:420
  32.2 0.7 %copy.14 = bf16[128,512]{1,0:T(8,128)(2,1)} copy(bf16[128,512]{1,0:T(8,128)(2,1)S(1)} %get-tuple-element.2) | data formatting | bytes 262144
  32.9 0.6 %copy.15 = bf16[128,256]{1,0:T(8,128)(2,1)} copy(bf16[128,256]{1,0:T(8,128)(2,1)S(1)} %get-tuple-element.3) | data formatting | bytes 131072

commit v6 on v5

--- a/solution.py
+++ b/solution.py
@@ -12,6 +12,7 @@
 BF16 = jnp.bfloat16
 CORES = 2
 BLOCK = 32
+LOG2_E = 1.4426950408889634
 ARGS = 10
 PIECES = 2
 AHEAD = 4
@@ -177,46 +178,56 @@
 
     for at in LOAD_ORDER[4:]:
         loads[at].wait()
+    query = dequant_rows(q_ref[...], qe_ref[...])
     kv = dequant_rows(kv_ref[...], kve_ref[...])
+    grad = dequant_rows(do_ref[...], doe_ref[...])
     keys, values = kv[:, :size], kv[:, size:]
     block = CORES * tokens
-    key_at = lax.broadcasted_iota(jnp.int32, (seq, block), 0)
-    query_at = lax.broadcasted_iota(jnp.int32, (seq, block), 1)
+    visible = lax.broadcasted_iota(jnp.int32, (block, block), 0) <= lax.broadcasted_iota(
+        jnp.int32, (block, block), 1
+    )
     dq_copies = []
-    for k in [*range(1, chips), 0]:
-        first = pl.multiple_of(lax.rem(y + k, chips) * block, block)
-        at = pl.ds(first, block)
-        q_block = dequant_rows(q_ref[at, :], qe_ref[:, at])
-        do_block = dequant_rows(do_ref[at, :], doe_ref[:, at])
-        scores = dot_nt(keys, q_block)
-        scores = jnp.where(key_at <= first + query_at, scores, -jnp.inf)
-        expd = jnp.exp((scores - jnp.max(scores, axis=0, keepdims=True)) * scale)
-        probs = expd * (1.0 / jnp.sum(expd, axis=0, keepdims=True))
-        probs_b = probs.astype(BF16)
-        dprob = dot_nt(values, do_block)
-        delta = jnp.sum(probs_b.astype(F32) * dprob, axis=0, keepdims=True)
-        dscore = (probs * (dprob - delta) * scale).astype(BF16)
-        dq_pair[at, :size] = dot_tn(dscore, keys).astype(BF16)
+    for index in reversed(range(chips)):
+        first, upper = index * block, (index + 1) * block
+        q_block, do_block = query[first:upper], grad[first:upper]
+        spans = [(first, upper)] + ([(0, first)] if first else [])
+        scores = [dot_nt(keys[lo:hi], q_block) for lo, hi in spans]
+        scores[0] = jnp.where(visible, scores[0], -jnp.inf)
+        peak = functools.reduce(
+            jnp.maximum, [jnp.max(part, axis=0, keepdims=True) for part in scores]
+        )
+        expd = [jnp.exp2((part - peak) * (scale * LOG2_E)) for part in scores]
+        total = sum(jnp.sum(part, axis=0, keepdims=True) for part in expd)
+        inverse = 1.0 / total
+        probs = [part * inverse for part in expd]
+        dprob = [dot_nt(values[lo:hi], do_block) for lo, hi in spans]
+        delta = sum(
+            jnp.sum(p * dp, axis=0, keepdims=True) for p, dp in zip(probs, dprob)
+        )
+        dscore = [(p * (dp - delta)).astype(BF16) for p, dp in zip(probs, dprob)]
+        dq = sum(dot_tn(part, keys[lo:hi]) for part, (lo, hi) in zip(dscore, spans))
+        dq_pair[first:upper, :size] = (dq * scale).astype(BF16)
         copy = pltpu.make_async_remote_copy(
-            src_ref=dq_pair.at[at, pl.ds(0, size)],
-            dst_ref=dq_pair.at[at, pl.ds(size, size)],
-            send_sem=dq_send.at[k],
-            recv_sem=dq_recv.at[k],
+            src_ref=dq_pair.at[first:upper, :size],
+            dst_ref=dq_pair.at[first:upper, size:],
+            send_sem=dq_send.at[index],
+            recv_sem=dq_recv.at[index],
             device_id={"head": sibling},
             device_id_type=MESH,
         )
         copy.start()
         dq_copies.append(copy)
-        dk = jnp.dot(dscore, q_block, preferred_element_type=F32)
-        dv = jnp.dot(probs_b, do_block, preferred_element_type=F32)
-        if len(dq_copies) == 1:
-            dk_acc[...] = dk
-            dv_acc[...] = dv
-        else:
-            dk_acc[...] += dk
-            dv_acc[...] += dv
-
-    dkv_out[:, :size] = dk_acc[...].astype(BF16)
+        for part, p, (lo, hi) in zip(dscore, probs, spans):
+            dk = jnp.dot(part, q_block, preferred_element_type=F32)
+            dv = jnp.dot(p.astype(BF16), do_block, preferred_element_type=F32)
+            if upper == seq:
+                dk_acc[lo:hi, :] = dk
+                dv_acc[lo:hi, :] = dv
+            else:
+                dk_acc[lo:hi, :] += dk
+                dv_acc[lo:hi, :] += dv
+
+    dkv_out[:, :size] = (dk_acc[...] * scale).astype(BF16)
     dkv_out[:, size:] = dv_acc[...].astype(BF16)
 
     def chip_rows(chip, core):
@@ -240,7 +251,7 @@
         return dot_nt(dq_pair[pl.ds(first, piece), :], wq_pair[pl.ds(at, wide), :])
 
     w_copy.wait_recv()
-    for copy in dq_copies[:-1]:
+    for copy in dq_copies:
         copy.wait_recv()
     chunks = [
         (i, core * PIECES + p)
@@ -288,7 +299,6 @@
 
     for i, e in chunks[AHEAD // 2 : AHEAD]:
         send_part(i, e)
-    dq_copies[-1].wait_recv()
 
     near_copies[-1].wait_recv()
     total = dkv_out[chip_rows(y, c), :].astype(F32) + dkv_near[0].astype(F32)

time: 33.7 us -> 33.7 us (level)
  no operation moved by 1% of the time
where the time goes in v6:
time: 33.7 us; the launch traced here: 33.5 us
  Pallas kernels  31.6 us (94%)
  local copies, waits for them, and re-layouts  1.29 us (4%)
  between operations  0.64 us (2%)
    pallas_call x1, Pallas kernels, shards(): pl.pallas_call(functools.partial(kernel, groups, heads), out_shape=(pltpu...  31.6 us
    unnamed x2, local copies, waits for them, and re-layouts  1.29 us

profile of v6, /device:TPU:1, one launch (start us, length us, event | category | flops | bytes accessed | tf_op | source)
XLA Modules:
  0.0 33.5 jit_solution(13426235300350303269)
XLA Ops:
  0.6 31.6 %shard_map.113 = (bf16[128,512]{1,0:T(8,128)(2,1)S(1)}, bf16[128,256]{1,0:T(8,128)(2,1)S(1)}) custom-call(bf16[512,128]{1,0:T(8,128)(2,1)} %refs_0_.1, s32[4,512]{1,0:T(4,128)} %refs_1_.1, bf16[512,256]{1,0:T(8,128)(2,1)} %refs_2_.1, s32[8,512]{1,0:T(8,128)} %refs_3_.1, bf16[512,128]{1,0:T(8,128)(2,1)} %refs_4_.1, s32[4,512]{1,0:T(4,128)} %refs_5_.1, ...), custom_call_target="tpu_custom_call" | custom-call | tf_op jit(solution)/shard_map/pallas_call | solution.py:430
  32.2 0.7 %copy.14 = bf16[128,512]{1,0:T(8,128)(2,1)} copy(bf16[128,512]{1,0:T(8,128)(2,1)S(1)} %get-tuple-element.2) | data formatting | bytes 262144
  32.9 0.6 %copy.15 = bf16[128,256]{1,0:T(8,128)(2,1)} copy(bf16[128,256]{1,0:T(8,128)(2,1)S(1)} %get-tuple-element.3) | data formatting | bytes 131072

commit v7 on v6

--- a/solution.py
+++ b/solution.py
@@ -186,7 +186,11 @@
     visible = lax.broadcasted_iota(jnp.int32, (block, block), 0) <= lax.broadcasted_iota(
         jnp.int32, (block, block), 1
     )
-    dq_copies = []
+    dq_copies, near_copies = [], []
+
+    def chip_rows(chip, core):
+        return pl.ds(pl.multiple_of((chip * CORES + core) * tokens, tokens), tokens)
+
     for index in reversed(range(chips)):
         first, upper = index * block, (index + 1) * block
         q_block, do_block = query[first:upper], grad[first:upper]
@@ -205,6 +209,28 @@
             jnp.sum(p * dp, axis=0, keepdims=True) for p, dp in zip(probs, dprob)
         )
         dscore = [(p * (dp - delta)).astype(BF16) for p, dp in zip(probs, dprob)]
+        for part, p, (lo, hi) in zip(dscore, probs, spans):
+            dk = jnp.dot(part, q_block, preferred_element_type=F32)
+            dv = jnp.dot(p.astype(BF16), do_block, preferred_element_type=F32)
+            if upper == seq:
+                dk_acc[lo:hi, :] = dk
+                dv_acc[lo:hi, :] = dv
+            else:
+                dk_acc[lo:hi, :] += dk
+                dv_acc[lo:hi, :] += dv
+
+        dkv_out[first:upper, :size] = (dk_acc[first:upper, :] * scale).astype(BF16)
+        dkv_out[first:upper, size:] = dv_acc[first:upper, :].astype(BF16)
+        copy = pltpu.make_async_remote_copy(
+            src_ref=dkv_out.at[chip_rows(index, 1 - c)],
+            dst_ref=dkv_near.at[index],
+            send_sem=near_send.at[index],
+            recv_sem=near_recv.at[index],
+            device_id={"head": sibling},
+            device_id_type=MESH,
+        )
+        copy.start()
+        near_copies.append(copy)
         dq = sum(dot_tn(part, keys[lo:hi]) for part, (lo, hi) in zip(dscore, spans))
         dq_pair[first:upper, :size] = (dq * scale).astype(BF16)
         copy = pltpu.make_async_remote_copy(
@@ -217,34 +243,25 @@
         )
         copy.start()
         dq_copies.append(copy)
-        for part, p, (lo, hi) in zip(dscore, probs, spans):
-            dk = jnp.dot(part, q_block, preferred_element_type=F32)
-            dv = jnp.dot(p.astype(BF16), do_block, preferred_element_type=F32)
-            if upper == seq:
-                dk_acc[lo:hi, :] = dk
-                dv_acc[lo:hi, :] = dv
-            else:
-                dk_acc[lo:hi, :] += dk
-                dv_acc[lo:hi, :] += dv
-
-    dkv_out[:, :size] = (dk_acc[...] * scale).astype(BF16)
-    dkv_out[:, size:] = dv_acc[...].astype(BF16)
-
-    def chip_rows(chip, core):
-        return pl.ds(pl.multiple_of((chip * CORES + core) * tokens, tokens), tokens)
-
-    near_copies = []
-    for k in [*range(1, chips), 0]:
+
+    for copy in near_copies:
+        copy.wait_recv()
+    dkv_copies = []
+    for k in range(1, chips):
+        to = lax.rem(y + k, chips)
+        both = dkv_out[chip_rows(to, c), :].astype(F32) + dkv_near[to].astype(F32)
+        dkv_sum[k - 1] = both.astype(BF16)
         copy = pltpu.make_async_remote_copy(
-            src_ref=dkv_out.at[chip_rows(lax.rem(y + k, chips), 1 - c)],
-            dst_ref=dkv_near.at[k],
-            send_sem=near_send.at[k],
-            recv_sem=near_recv.at[k],
-            device_id={"head": sibling},
+            src_ref=dkv_sum.at[k - 1],
+            dst_ref=dkv_in.at[k - 1],
+            send_sem=dkv_send.at[k - 1],
+            recv_sem=dkv_recv.at[k - 1],
+            device_id={"head": to * CORES + c},
             device_id_type=MESH,
         )
         copy.start()
-        near_copies.append(copy)
+        dkv_copies.append(copy)
+
     def q_term(chip, b, e):
         first = pl.multiple_of(chip * CORES * tokens + e * piece, piece)
         at = pl.multiple_of(b * wide, wide)
@@ -277,31 +294,10 @@
             copy.start()
             part_copies[k, i, e] = copy
 
-    for i, e in chunks[: AHEAD // 2]:
+    for i, e in chunks[:AHEAD]:
         send_part(i, e)
 
-    dkv_copies = []
-    for k in range(1, chips):
-        to = lax.rem(y + k, chips)
-        near_copies[k - 1].wait_recv()
-        both = dkv_out[chip_rows(to, c), :].astype(F32) + dkv_near[k].astype(F32)
-        dkv_sum[k - 1] = both.astype(BF16)
-        copy = pltpu.make_async_remote_copy(
-            src_ref=dkv_sum.at[k - 1],
-            dst_ref=dkv_in.at[k - 1],
-            send_sem=dkv_send.at[k - 1],
-            recv_sem=dkv_recv.at[k - 1],
-            device_id={"head": to * CORES + c},
-            device_id_type=MESH,
-        )
-        copy.start()
-        dkv_copies.append(copy)
-
-    for i, e in chunks[AHEAD // 2 : AHEAD]:
-        send_part(i, e)
-
-    near_copies[-1].wait_recv()
-    total = dkv_out[chip_rows(y, c), :].astype(F32) + dkv_near[0].astype(F32)
+    total = dkv_out[chip_rows(y, c), :].astype(F32) + dkv_near[y].astype(F32)
     for k in range(1, chips):
         dkv_copies[k - 1].wait_recv()
         total = total + dkv_in[k - 1].astype(F32)

time: 33.7 us -> 32.2 us (0.955)
  Pallas kernels: 31.6 us -> 30.1 us
    pallas_call x1, Pallas kernels: 31.6 us -> 30.1 us  [shards(): pl.pallas_call(functools.partial(kernel, groups, heads), out_shape=(pltpu...]
where the time goes in v7:
time: 32.2 us; the launch traced here: 32.1 us
  Pallas kernels  30.1 us (93%)
  local copies, waits for them, and re-layouts  1.29 us (4%)
  between operations  0.64 us (2%)
    pallas_call x1, Pallas kernels, shards(): pl.pallas_call(functools.partial(kernel, groups, heads), out_shape=(pltpu...  30.1 us
    unnamed x2, local copies, waits for them, and re-layouts  1.29 us

profile of v7, /device:TPU:1, one launch (start us, length us, event | category | flops | bytes accessed | tf_op | source)
XLA Modules:
  0.0 32.1 jit_solution(8560926193567440639)
XLA Ops:
  0.6 30.1 %shard_map.113 = (bf16[128,512]{1,0:T(8,128)(2,1)S(1)}, bf16[128,256]{1,0:T(8,128)(2,1)S(1)}) custom-call(bf16[512,128]{1,0:T(8,128)(2,1)} %refs_0_.1, s32[4,512]{1,0:T(4,128)} %refs_1_.1, bf16[512,256]{1,0:T(8,128)(2,1)} %refs_2_.1, s32[8,512]{1,0:T(8,128)} %refs_3_.1, bf16[512,128]{1,0:T(8,128)(2,1)} %refs_4_.1, s32[4,512]{1,0:T(4,128)} %refs_5_.1, ...), custom_call_target="tpu_custom_call" | custom-call | tf_op jit(solution)/shard_map/pallas_call | solution.py:426
  30.8 0.7 %copy.14 = bf16[128,512]{1,0:T(8,128)(2,1)} copy(bf16[128,512]{1,0:T(8,128)(2,1)S(1)} %get-tuple-element.2) | data formatting | bytes 262144
  31.4 0.6 %copy.15 = bf16[128,256]{1,0:T(8,128)(2,1)} copy(bf16[128,256]{1,0:T(8,128)(2,1)S(1)} %get-tuple-element.3) | data formatting | bytes 131072

commit v8 on v7

--- a/solution.py
+++ b/solution.py
@@ -140,23 +140,31 @@
     pl.semaphore_wait(barrier, heads - 1 + CORES * (groups - 1))
 
     my_half = h // owners
-    my_slot = pl.multiple_of(lax.rem(h, owners) * rows, rows)
-
-    def wkv_copy(j):
+    my_owner = lax.rem(h, owners)
+    my_slot = pl.multiple_of(my_owner * rows, rows)
+    early = (my_owner * rows) // wide == lax.rem(z + 1, per_half)
+
+    def wkv_copy(j, part):
+        cut = rows // 2
+        at = pl.multiple_of(my_owner * rows + part * cut, cut)
         return pltpu.make_async_remote_copy(
-            src_ref=wkv_out,
-            dst_ref=wkv_half.at[pl.ds(my_slot, rows)],
-            send_sem=wkv_send.at[j],
-            recv_sem=wkv_recv.at[lax.rem(h, owners)],
+            src_ref=wkv_out.at[pl.ds(part * cut, cut)],
+            dst_ref=wkv_half.at[pl.ds(at, cut)],
+            send_sem=wkv_send.at[j, part],
+            recv_sem=wkv_recv.at[my_owner, part],
             device_id={"head": CORES * j + my_half},
             device_id_type=MESH,
         )
 
-    for j in range(owners):
-
-        @pl.when(CORES * j + my_half != h)
-        def _():
-            wkv_copy(j).start()
+    def send_wkv(part, now):
+        for j in range(owners):
+
+            @pl.when(jnp.logical_and(CORES * j + my_half != h, now))
+            def _():
+                wkv_copy(j, part).start()
+
+    send_wkv(0, True)
+    send_wkv(1, early)
 
     for at in LOAD_ORDER[2:4]:
         loads[at].wait()
@@ -261,6 +269,8 @@
         )
         copy.start()
         dkv_copies.append(copy)
+
+    send_wkv(1, jnp.logical_not(early))
 
     def q_term(chip, b, e):
         first = pl.multiple_of(chip * CORES * tokens + e * piece, piece)
@@ -313,19 +323,6 @@
         device_id_type=MESH,
     )
     kvg_copy.start()
-    for s in range(owners):
-
-        @pl.when(c * owners + s != h)
-        def _():
-            pltpu.make_async_remote_copy(
-                src_ref=wkv_out,
-                dst_ref=wkv_half.at[pl.ds(s * rows, rows)],
-                send_sem=wkv_send.at[s],
-                recv_sem=wkv_recv.at[s],
-                device_id={"head": sibling},
-                device_id_type=MESH,
-            ).wait_recv()
-
     pltpu.make_async_remote_copy(
         src_ref=kvg_pair.at[c],
         dst_ref=kvg_pair.at[1 - c],
@@ -349,6 +346,22 @@
         b = lax.rem(z + 1 + i, per_half)
         to_z = c * per_half + b
         at = pl.multiple_of(b * wide, wide)
+        if n % (CORES * PIECES) == 0:
+            for s in range(owners):
+
+                @pl.when(jnp.logical_and(c * owners + s != h, (s * rows) // wide == b))
+                def _():
+                    for part in range(2):
+                        cut = rows // 2
+                        pltpu.make_async_remote_copy(
+                            src_ref=wkv_out.at[pl.ds(part * cut, cut)],
+                            dst_ref=wkv_half.at[pl.ds(s * rows + part * cut, cut)],
+                            send_sem=wkv_send.at[s, part],
+                            recv_sem=wkv_recv.at[s, part],
+                            device_id={"head": sibling},
+                            device_id_type=MESH,
+                        ).wait_recv()
+
         acc = q_term(y, b, e)
         kvg_piece = kvg_pair[e // PIECES, pl.ds(e % PIECES * piece, piece), :]
         acc = acc + dot_nt(kvg_piece, wkv_half[pl.ds(at, wide), :])
@@ -395,7 +408,8 @@
 
         @pl.when(CORES * j + my_half != h)
         def _():
-            wkv_copy(j).wait_send()
+            wkv_copy(j, 0).wait_send()
+            wkv_copy(j, 1).wait_send()
 
     for copy in [w_copy, *dq_copies, kvg_copy, *near_copies, *dkv_copies]:
         copy.wait_send()
@@ -451,8 +465,8 @@
             pltpu.VMEM((seq, size), F32),
             pltpu.VMEM((seq, size), F32),
             dma((2,)),
-            dma((owners,)),
-            dma((owners,)),
+            dma((owners, 2)),
+            dma((owners, 2)),
             dma((chips,)),
             dma((chips,)),
             dma((chips,)),

time: 32.2 us -> 31.7 us (0.984)
  Pallas kernels: 30.1 us -> 29.6 us
    pallas_call x1, Pallas kernels: 30.1 us -> 29.6 us  [shards(): pl.pallas_call(functools.partial(kernel, groups, heads), out_shape=(pltpu...]
where the time goes in v8:
time: 31.7 us; the launch traced here: 31.5 us
  Pallas kernels  29.6 us (93%)
  local copies, waits for them, and re-layouts  1.29 us (4%)
  between operations  0.64 us (2%)
    pallas_call x1, Pallas kernels, shards(): pl.pallas_call(functools.partial(kernel, groups, heads), out_shape=(pltpu...  29.6 us
    unnamed x2, local copies, waits for them, and re-layouts  1.29 us

profile of v8, /device:TPU:1, one launch (start us, length us, event | category | flops | bytes accessed | tf_op | source)
XLA Modules:
  0.0 31.5 jit_solution(9978389358964635033)
XLA Ops:
  0.6 29.6 %shard_map.113 = (bf16[128,512]{1,0:T(8,128)(2,1)S(1)}, bf16[128,256]{1,0:T(8,128)(2,1)S(1)}) custom-call(bf16[512,128]{1,0:T(8,128)(2,1)} %refs_0_.1, s32[4,512]{1,0:T(4,128)} %refs_1_.1, bf16[512,256]{1,0:T(8,128)(2,1)} %refs_2_.1, s32[8,512]{1,0:T(8,128)} %refs_3_.1, bf16[512,128]{1,0:T(8,128)(2,1)} %refs_4_.1, s32[4,512]{1,0:T(4,128)} %refs_5_.1, ...), custom_call_target="tpu_custom_call" | custom-call | tf_op jit(solution)/shard_map/pallas_call | solution.py:440
  30.2 0.7 %copy.14 = bf16[128,512]{1,0:T(8,128)(2,1)} copy(bf16[128,512]{1,0:T(8,128)(2,1)S(1)} %get-tuple-element.2) | data formatting | bytes 262144
  30.9 0.6 %copy.15 = bf16[128,256]{1,0:T(8,128)(2,1)} copy(bf16[128,256]{1,0:T(8,128)(2,1)S(1)} %get-tuple-element.3) | data formatting | bytes 131072

commit v9 on v8

--- a/solution.py
+++ b/solution.py
@@ -14,8 +14,8 @@
 BLOCK = 32
 LOG2_E = 1.4426950408889634
 ARGS = 10
-PIECES = 2
-AHEAD = 4
+PIECES = 4
+AHEAD = 8
 LOAD_ORDER = (8, 9, 6, 7, 0, 1, 2, 3, 4, 5)
 
 

time: 31.7 us -> 31.5 us (level)
  Pallas kernels: 29.6 us -> 29.2 us
    pallas_call x1, Pallas kernels: 29.6 us -> 29.2 us  [shards(): pl.pallas_call(functools.partial(kernel, groups, heads), out_shape=(pltpu...]
where the time goes in v9:
time: 31.5 us; the launch traced here: 31.1 us
  Pallas kernels  29.2 us (93%)
  local copies, waits for them, and re-layouts  1.29 us (4%)
  between operations  0.64 us (2%)
    pallas_call x1, Pallas kernels, shards(): pl.pallas_call(functools.partial(kernel, groups, heads), out_shape=(pltpu...  29.2 us
    unnamed x2, local copies, waits for them, and re-layouts  1.29 us

profile of v9, /device:TPU:1, one launch (start us, length us, event | category | flops | bytes accessed | tf_op | source)
XLA Modules:
  0.0 31.1 jit_solution(505646055251004973)
XLA Ops:
  0.6 29.2 %shard_map.113 = (bf16[128,512]{1,0:T(8,128)(2,1)S(1)}, bf16[128,256]{1,0:T(8,128)(2,1)S(1)}) custom-call(bf16[512,128]{1,0:T(8,128)(2,1)} %refs_0_.1, s32[4,512]{1,0:T(4,128)} %refs_1_.1, bf16[512,256]{1,0:T(8,128)(2,1)} %refs_2_.1, s32[8,512]{1,0:T(8,128)} %refs_3_.1, bf16[512,128]{1,0:T(8,128)(2,1)} %refs_4_.1, s32[4,512]{1,0:T(4,128)} %refs_5_.1, ...), custom_call_target="tpu_custom_call" | custom-call | tf_op jit(solution)/shard_map/pallas_call | solution.py:440
  29.8 0.7 %copy.14 = bf16[128,512]{1,0:T(8,128)(2,1)} copy(bf16[128,512]{1,0:T(8,128)(2,1)S(1)} %get-tuple-element.2) | data formatting | bytes 262144
  30.5 0.6 %copy.15 = bf16[128,256]{1,0:T(8,128)(2,1)} copy(bf16[128,256]{1,0:T(8,128)(2,1)S(1)} %get-tuple-element.3) | data formatting | bytes 131072

commit v10 on v8

--- a/solution.py
+++ b/solution.py
@@ -270,8 +270,6 @@
         copy.start()
         dkv_copies.append(copy)
 
-    send_wkv(1, jnp.logical_not(early))
-
     def q_term(chip, b, e):
         first = pl.multiple_of(chip * CORES * tokens + e * piece, piece)
         at = pl.multiple_of(b * wide, wide)
@@ -306,6 +304,8 @@
 
     for i, e in chunks[:AHEAD]:
         send_part(i, e)
+
+    send_wkv(1, jnp.logical_not(early))
 
     total = dkv_out[chip_rows(y, c), :].astype(F32) + dkv_near[y].astype(F32)
     for k in range(1, chips):

time: 31.7 us -> 31.3 us (0.987)
  Pallas kernels: 29.6 us -> 29.2 us
    pallas_call x1, Pallas kernels: 29.6 us -> 29.2 us  [shards(): pl.pallas_call(functools.partial(kernel, groups, heads), out_shape=(pltpu...]
where the time goes in v10:
time: 31.3 us; the launch traced here: 31.2 us
  Pallas kernels  29.2 us (93%)
  local copies, waits for them, and re-layouts  1.29 us (4%)
  between operations  0.64 us (2%)
    pallas_call x1, Pallas kernels, shards(): pl.pallas_call(functools.partial(kernel, groups, heads), out_shape=(pltpu...  29.2 us
    unnamed x2, local copies, waits for them, and re-layouts  1.29 us

profile of v10, /device:TPU:1, one launch (start us, length us, event | category | flops | bytes accessed | tf_op | source)
XLA Modules:
  0.0 31.2 jit_solution(16761082124820561736)
XLA Ops:
  0.6 29.2 %shard_map.113 = (bf16[128,512]{1,0:T(8,128)(2,1)S(1)}, bf16[128,256]{1,0:T(8,128)(2,1)S(1)}) custom-call(bf16[512,128]{1,0:T(8,128)(2,1)} %refs_0_.1, s32[4,512]{1,0:T(4,128)} %refs_1_.1, bf16[512,256]{1,0:T(8,128)(2,1)} %refs_2_.1, s32[8,512]{1,0:T(8,128)} %refs_3_.1, bf16[512,128]{1,0:T(8,128)(2,1)} %refs_4_.1, s32[4,512]{1,0:T(4,128)} %refs_5_.1, ...), custom_call_target="tpu_custom_call" | custom-call | tf_op jit(solution)/shard_map/pallas_call | solution.py:440
  29.9 0.7 %copy.14 = bf16[128,512]{1,0:T(8,128)(2,1)} copy(bf16[128,512]{1,0:T(8,128)(2,1)S(1)} %get-tuple-element.2) | data formatting | bytes 262144
  30.5 0.6 %copy.15 = bf16[128,256]{1,0:T(8,128)(2,1)} copy(bf16[128,256]{1,0:T(8,128)(2,1)S(1)} %get-tuple-element.3) | data formatting | bytes 131072
